TPU v7x, 32 devices: a whole 2x2x4 slice. The times are simulated.
32 devices in a mesh: groups: 2 (over x), tp: 16 (over z, y, core).
Axes of the slice: x: 2, y: 2, z: 4, core: 2. Of those that a mesh axis runs over, the one named last changes fastest.
Arguments:
- queries: bfloat16 [256, 8192], P(('groups', 'tp')), parts along dimension 0, may hold values from -6 to 6
- cache_kv: bfloat16 [256, 256, 2048], P(('groups', 'tp')), parts along dimension 0, may hold values from -200 to 200
- cache_len: int32 [256], P(('groups', 'tp')), parts along dimension 0, may hold values from 2 to 256, as said below
- image_kv: bfloat16 [16384, 2048], P(('groups', 'tp')), parts along dimension 0, may hold values from -6 to 6
- row_request: int32 [16384, 1], P('groups'), parts along dimension 0, may hold values from 0 to 127; in each aligned block of 512 rows (0 to 511, 512 to 1023, ...) at most 8 rows name the same one
- slot_of_request: int32 [256], P('groups'), parts along dimension 0, may hold values from 0 to 127, each once
- out_weight: bfloat16 [8192, 8192], P('tp'), may hold values from -0.59765625 to 0.59765625
Outputs:
- projected: bfloat16 [256, 8192], P(('groups', 'tp')), parts along dimension 0
There are 2 independent parts, one for each index of `groups`. A program takes and returns all parts, laid end to end along the dimension named above; an argument that names none is the same for every part. Nothing has to cross between parts.
Inputs may be any that keep to these rules, and one draw needn't show every extreme that they name: `row_request`: the rows of one device, 512 rows in order, name one request at most 8 times, a bound that some block reaches. `slot_of_request`: each slot once. `cache_len`: some slot holds exactly 256.
All inputs are finite; a program needn't handle non-finite values.
Results may differ from a plain program's by a relative error of at most 0.0055.
Values may be sent and summed in bfloat16 or wider, within the bound.
A program may use at most 128 MiB of HBM per device.

v0:
```python
import math

import jax
import jax.numpy as jnp
from jax import lax
from jax.sharding import PartitionSpec as P

QH = 64
KVH = 8
HD = 128
CACHE = 256


low_fill = -1e30


def softmax_part(scores, live_mask, floor_top):
    masked = jnp.where(live_mask, scores, low_fill)
    highest = jnp.maximum(floor_top, jnp.max(masked, axis=-1))
    weights = jnp.where(live_mask, jnp.exp(scores - highest[..., None]), 0.0).astype(jnp.bfloat16)
    weight_sums = jnp.sum(weights.astype(jnp.float32), axis=-1)
    return (highest, weights, weight_sums)


def per_device(queries, cache_kv, cache_len, image_kv, row_request, slot_of_request, out_weight):
    tp_size = lax.axis_size("tp")
    my_index = lax.axis_index("tp")
    local_req = queries.shape[0]
    all_req = local_req * tp_size
    img_local = image_kv.shape[0]
    kv_width = KVH * HD
    capacity = max(2, (2 * img_local + all_req - 1) // all_req)
    score_scale = 1.0 / math.sqrt(HD)
    req_iota = jnp.arange(all_req, dtype=jnp.int32)
    my_rows = lax.dynamic_slice_in_dim(row_request[:, 0], my_index * img_local, img_local)
    row_slot = jnp.sum(
        jnp.where(my_rows[:, None] == req_iota[None, :], slot_of_request[None, :], 0), axis=1
    )
    row_iota = jnp.arange(img_local, dtype=jnp.int32)
    earlier = (my_rows[:, None] == my_rows[None, :]) & (row_iota[None, :] < row_iota[:, None])
    row_rank = jnp.sum(earlier.astype(jnp.int32), axis=1)
    bucket = jnp.zeros((all_req * capacity, 2 * kv_width), jnp.bfloat16)
    bucket = bucket.at[row_slot * capacity + row_rank].set(image_kv)
    bucket = bucket.reshape(all_req, capacity, 2 * kv_width)
    arrived = lax.all_to_all(bucket, "tp", split_axis=0, concat_axis=1, tiled=True)
    grouped = queries.reshape(local_req, KVH, QH // KVH, HD)
    cache_keys = cache_kv[:, :, :kv_width].reshape(local_req, CACHE, KVH, HD)
    cache_vals = cache_kv[:, :, kv_width:].reshape(local_req, CACHE, KVH, HD)
    cache_scores = (
        jnp.einsum("rgjd,rpgd->rgjp", grouped, cache_keys, preferred_element_type=jnp.float32)
        * score_scale
    )
    cache_live = (jnp.arange(CACHE, dtype=jnp.int32)[None, :] < cache_len[:, None])[
        :, None, None, :
    ]
    cache_top, cache_weights, cache_sum = softmax_part(cache_scores, cache_live, low_fill)
    cache_num = jnp.einsum(
        "rgjp,rpgd->rgjd", cache_weights, cache_vals, preferred_element_type=jnp.float32
    )
    my_slots = my_index * local_req + jnp.arange(local_req, dtype=jnp.int32)
    owned_slot = slot_of_request[:, None] == my_slots[None, :]
    my_requests = jnp.sum(jnp.where(owned_slot, req_iota[:, None], 0), axis=0)
    matches = (row_request[:, 0][:, None] == my_requests[None, :]).astype(jnp.int32)
    counts = jnp.sum(matches.reshape(tp_size, img_local, local_req), axis=1)
    rank_iota = jnp.arange(capacity, dtype=jnp.int32)
    image_live = rank_iota[None, :, None] < counts[:, None, :]
    image_live = jnp.transpose(image_live, (2, 0, 1)).reshape(local_req, tp_size * capacity)[
        :, None, None, :
    ]
    image_keys = arrived[:, :, :kv_width].reshape(local_req, tp_size * capacity, KVH, HD)
    image_vals = arrived[:, :, kv_width:].reshape(local_req, tp_size * capacity, KVH, HD)
    image_scores = (
        jnp.einsum("rgjd,rsgd->rgjs", grouped, image_keys, preferred_element_type=jnp.float32)
        * score_scale
    )
    image_top, image_weights, image_sum = softmax_part(image_scores, image_live, cache_top)
    image_num = jnp.einsum(
        "rgjs,rsgd->rgjd", image_weights, image_vals, preferred_element_type=jnp.float32
    )
    factor = jnp.exp(cache_top - image_top)
    attended = (cache_num * factor[..., None] + image_num) / (cache_sum * factor + image_sum)[
        ..., None
    ]
    attended = attended.reshape(local_req, QH * HD).astype(jnp.bfloat16)
    by_head = lax.all_to_all(attended, "tp", split_axis=1, concat_axis=0, tiled=True)
    summed = lax.psum_scatter(
        jnp.dot(by_head, out_weight, preferred_element_type=jnp.float32),
        "tp",
        scatter_dimension=0,
        tiled=True,
    )
    return summed.astype(jnp.bfloat16)


def solution(mesh):
    placed = (
        P(("groups", "tp"), None),
        P(("groups", "tp"), None, None),
        P(("groups", "tp")),
        P(("groups", "tp"), None),
        P("groups", None),
        P("groups"),
        P("tp", None),
    )
    return jax.shard_map(
        per_device, mesh=mesh, in_specs=placed, out_specs=P(("groups", "tp"), None), check_vma=False
    )
```

profile of v0, /device:TPU:0, one launch (start us, length us, event | category | flops | bytes accessed | tf_op | source)
XLA Modules:
  0.0 233.4 jit_solution(6575200419707800195)
XLA Ops:
  6.5 0.7 constant_dynamic-slice_fusion
  7.2 0.3 convert_reduce_fusion
  7.5 0.9 select_reduce_fusion.2
  8.4 7.3 %scatter_custom_fusion = bf16[1024,2048]{1,0:T(8,128)(2,1)} fusion(s32[512]{0:T(512)S(1)} %bitcast.42, bf16[512,2048]{1,0:T(8,128)(2,1)} %param.10, bf16[]{:T(256)} %constant.4.clone.1), kind=kCustom, calls=%fused_computation.2 | custom fusion | bytes 4194816 | tf_op jit(solution)/shard_map/scatter | solution.py:43
  15.6 7.6 %all-to-all-start = ((bf16[128,8,2048]{2,1,0:T(8,128)(2,1)}), bf16[128,8,2048]{2,1,0:T(8,128)(2,1)}, u32[]{:S(2)}, u32[]{:S(2)}) async-start(bf16[128,8,2048]{2,1,0:T(8,128)(2,1)} %bitcast.30), calls=%async_computation | async-start | bytes 8388608 | tf_op jit(solution)/shard_map/all_to_all | solution.py:45
  23.2 0.2 reduce-scatter.2.cloned.1.call-start
  23.5 0.1 lt.76
  23.6 0.5 broadcast.79
  24.1 0.7 reduce.5
  24.8 0.2 select_reduce_fusion.3
  25.0 0.4 convert_reduce_fusion.3
  25.6 0.1 lt.80
  25.7 5.9 %fusion.12 = (bf16[8,256,1024]{2,1,0:T(8,128)(2,1)}, bf16[8,256,1024]{2,1,0:T(8,128)(2,1)}) fusion(bf16[8,256,2048]{2,1,0:T(8,128)(2,1)} %param.8), kind=kLoop, calls=%fused_computation.39 | loop fusion | bytes 16777216 | tf_op jit(solution)/shard_map/slice | solution.py:47
  31.6 6.4 %copy.50 = bf16[8,256,1024]{1,2,0:T(8,128)(2,1)} copy(bf16[8,256,1024]{2,1,0:T(8,128)(2,1)} %get-tuple-element.7) | data formatting | bytes 8388608
  38.1 6.5 %copy.51 = bf16[8,256,1024]{1,2,0:T(8,128)(2,1)} copy(bf16[8,256,1024]{2,1,0:T(8,128)(2,1)} %get-tuple-element.8) | data formatting | bytes 8388608
  44.7 2.9 %select_reduce_fusion = (f32[8,8,8]{2,1,0:T(8,128)S(1)}, f32[8,8,8,256]{3,2,1,0:T(8,128)S(1)}) fusion(pred[8,256]{1,0:T(8,128)(4,1)S(1)} %iota_compare_fusion.2, bf16[8,256,8,128]{1,3,2,0:T(8,128)(2,1)} %bitcast.32, bf16[8,8,8,128]{3,0,2,1:T(8,128)(2,1)S(1)} %bitcast.36), kind=kOutput, calls=%fused_computation.15 | convolution fusion | flops 33947136 | bytes 4853760 | tf_op jit(solution)/shard_map/rgjd,rpgd->rgjp/dot_general | solution.py:50
  47.6 53.3 %all-to-all-done = bf16[128,8,2048]{2,1,0:T(8,128)(2,1)} async-done(((bf16[128,8,2048]{2,1,0:T(8,128)(2,1)}), bf16[128,8,2048]{2,1,0:T(8,128)(2,1)}, u32[]{:S(2)}, u32[]{:S(2)}) %all-to-all-start) | async-done | bytes 4194336 | tf_op jit(solution)/shard_map/all_to_all | solution.py:45
  100.9 2.5 %copy.61 = bf16[8,16,8,2048]{3,2,1,0:T(8,128)(2,1)S(1)} copy(bf16[8,16,8,2048]{3,2,0,1:T(8,128)(2,1)} %bitcast.9) | data formatting | bytes 8388608 | tf_op jit(solution)/shard_map/all_to_all | solution.py:45
  103.4 2.4 %fusion.13 = (bf16[8,128,1024]{2,1,0:T(8,128)(2,1)}, bf16[8,128,1024]{2,1,0:T(8,128)(2,1)}) fusion(bf16[8,128,2048]{2,1,0:T(8,128)(2,1)S(1)} %bitcast.33), kind=kLoop, calls=%fused_computation.40 | loop fusion | bytes 8388608 | tf_op jit(solution)/shard_map/slice | solution.py:71
  105.8 3.0 %copy.43 = bf16[8,128,1024]{1,2,0:T(8,128)(2,1)S(1)} copy(bf16[8,128,1024]{2,1,0:T(8,128)(2,1)} %get-tuple-element.9) | data formatting | bytes 4194304 | tf_op jit(solution)/shard_map/slice | solution.py:71
  108.9 3.9 %copy.40 = bf16[8,128,1024]{1,2,0:T(8,128)(2,1)} copy(bf16[8,128,1024]{2,1,0:T(8,128)(2,1)} %get-tuple-element.10) | data formatting | bytes 4194304 | tf_op jit(solution)/shard_map/slice | solution.py:70
  112.8 2.3 select_reduce_fusion.1
  115.1 0.3 convert_reduce_fusion.1
  115.4 0.3 convert_reduce_fusion.2
  115.7 3.4 %convolution_multiply_fusion.2 = f32[8,8,8,128]{3,2,1,0:T(8,128)S(1)} fusion(bf16[8,256,8,128]{1,3,2,0:T(8,128)(2,1)} %bitcast.31, f32[8,8,8]{2,1,0:T(8,128)S(1)} %get-tuple-element.6, f32[8,8,8,256]{3,2,1,0:T(8,128)S(1)} %get-tuple-element.14, f32[8,8,8]{2,1,0:T(8,128)S(1)} %get-tuple-element.11, pred[8,256]{1,0:T(8,128)(4,1)S(1)} %iota_compare_fusion.2), kind=kOutput, calls=%fused_computation.8 | convolution fusion | flops 34013184 | bytes 4986880 | tf_op jit(solution)/shard_map/rgjp,rpgd->rgjd/dot_general | solution.py:57
  119.1 1.2 fusion.3
  120.4 0.1 convert_element_type.33
  120.5 0.1 copy.45
  120.6 27.4 %all_to_all.34 = bf16[8,16,512]{2,0,1:T(8,128)(2,1)S(1)} all-to-all(bf16[8,16,512]{2,0,1:T(8,128)(2,1)S(1)} %copy.45), channel_id=1, replica_groups=mesh['groups'=2,'tp'=16] {'tp'}, dimensions={1} | all-to-all | bytes 262144 | tf_op jit(solution)/shard_map/all_to_all | solution.py:85
  147.9 6.7 %fusion.5 = f32[128,8192]{1,0:T(8,128)} fusion(bf16[512,8192]{1,0:T(8,128)(2,1)} %param.13, bf16[8,16,512]{2,0,1:T(8,128)(2,1)S(1)} %all_to_all.34), kind=kOutput, calls=%fused_computation.22 | convolution fusion | flops 1073741824 | bytes 12713984 | tf_op jit(solution)/shard_map/dot_general | solution.py:87
  154.7 70.3 %reduce-scatter.2.cloned.1.call-done = f32[8,8192]{1,0:T(8,128)} async-done(((f32[128,8192]{1,0:T(8,128)}), f32[8,8192]{1,0:T(8,128)}) %reduce-scatter.2.cloned.1.call-update) | async-done | bytes 262160 | tf_op jit(solution)/shard_map/reduce_scatter | solution.py:86
  224.9 1.6 convert_element_type.34
  (20 shorter events, 0.3 us)
Async XLA Ops:
  15.6 8.4 %copy-start.1 = (s32[8192,1]{0,1:T(1,128)S(1)}, s32[8192,1]{0,1:T(1,128)}, u32[]{:S(2)}) copy-start(s32[8192,1]{0,1:T(1,128)} %param.11) | copy-start | bytes 98308
  15.6 9.2 %copy-start.2 = (s32[128]{0:T(128)S(1)}, s32[128]{0:T(128)}, u32[]{:S(2)}) copy-start(s32[128]{0:T(128)} %param.12) | copy-start | bytes 1540
  15.6 85.3 %all-to-all-start = ((bf16[128,8,2048]{2,1,0:T(8,128)(2,1)}), bf16[128,8,2048]{2,1,0:T(8,128)(2,1)}, u32[]{:S(2)}, u32[]{:S(2)}) async-start(bf16[128,8,2048]{2,1,0:T(8,128)(2,1)} %bitcast.30), calls=%async_computation | async-start | bytes 8388608 | tf_op jit(solution)/shard_map/all_to_all | solution.py:45
  23.2 201.7 %reduce-scatter.2.cloned.1.call-start = ((), (), s32[]{:S(2)}) async-start(), calls=%async_computation.3 | async-start | bytes 4456448 | tf_op jit(solution)/shard_map/reduce_scatter | solution.py:86
  38.1 6.5 %copy-start.3 = (s32[8]{0:T(128)S(1)}, s32[8]{0:T(128)}, u32[]{:S(2)}) copy-start(s32[8]{0:T(128)} %param.9) | copy-start | bytes 100
  38.1 6.6 %copy-start = (bf16[8,8192]{1,0:T(8,128)(2,1)S(1)}, bf16[8,8192]{1,0:T(8,128)(2,1)}, u32[]{:S(2)}) copy-start(bf16[8,8192]{1,0:T(8,128)(2,1)} %param.7) | copy-start | bytes 393220
Sparse Core Ops, SparseCore 0:
  154.8 70.0 reduce-scatter.1
where the time goes:
time: 234 us; the launch traced here: 233 us
  waiting for transfers between devices  124 us (53%)
  local copies, waits for them, and re-layouts  39.7 us (17%)
  blocking collectives  27.4 us (12%)
  matrix products  16.6 us (7%)
  between operations  13.5 us (6%)
  starting transfers between devices  7.79 us (3%)
  other arithmetic  4.75 us (2%)
    reduce_scatter x1, waiting for transfers between devices, per_device(): lax.psum_scatter(jnp.dot(by_head, out_weight, preferred_element_type=jnp....  70.3 us
    all_to_all x1, waiting for transfers between devices, per_device(): lax.all_to_all(bucket, 'tp', split_axis=0, concat_axis=1, tiled=True)  53.3 us
    all_to_all x1, blocking collectives, per_device(): lax.all_to_all(attended, 'tp', split_axis=1, concat_axis=0, tiled=True)  27.4 us
    unnamed x11, local copies, waits for them, and re-layouts  13.5 us
    all_to_all x1, starting transfers between devices, per_device(): lax.all_to_all(bucket, 'tp', split_axis=0, concat_axis=1, tiled=True)  7.57 us
    scatter x1, local copies, waits for them, and re-layouts, per_device(): bucket = bucket.at[row_slot * capacity + row_rank].set(image_kv)  7.26 us
    dot_general x1, matrix products, per_device(): jnp.dot(by_head, out_weight, preferred_element_type=jnp.float32)  6.69 us
    slice x1, local copies, waits for them, and re-layouts, per_device(): cache_keys = cache_kv[:, :, :kv_width].reshape(local_req, CACHE, KVH, HD)  5.93 us
  transfers between devices with their start and end apart: 2, of which 2 were waited for; matrix products, arithmetic and copies ran while one was open for 10% of the time, Pallas kernels for 0%

commit v1 on v0

v1 whole, which is shorter than its diff:
```python
import math

import jax
import jax.numpy as jnp
from jax import lax
from jax.sharding import PartitionSpec as P

QH = 64
KVH = 8
HD = 128

low_fill = -1e30


def per_device(queries, cache_kv, cache_len, image_kv, row_request, slot_of_request, out_weight):
    tp_size = lax.axis_size("tp")
    my_index = lax.axis_index("tp")
    local_req = queries.shape[0]
    cache = cache_kv.shape[1]
    all_req = local_req * tp_size
    img_local = image_kv.shape[0]
    kv_width = KVH * HD
    per_group = QH // KVH
    scale = 1.0 / math.sqrt(HD)
    all_q = lax.all_gather(queries, "tp", axis=0, tiled=True)

    grouped = queries.reshape(local_req, KVH, per_group, HD)
    cache_keys = cache_kv[:, :, :kv_width].reshape(local_req, cache, KVH, HD)
    cache_vals = cache_kv[:, :, kv_width:].reshape(local_req, cache, KVH, HD)
    cache_scores = (
        jnp.einsum("rgjd,rpgd->rgjp", grouped, cache_keys, preferred_element_type=jnp.float32) * scale
    )
    cache_live = (jnp.arange(cache, dtype=jnp.int32)[None, :] < cache_len[:, None])[:, None, None, :]
    cache_top = jnp.max(jnp.where(cache_live, cache_scores, low_fill), axis=-1)
    cache_w = jnp.where(cache_live, jnp.exp(cache_scores - cache_top[..., None]), 0.0).astype(jnp.bfloat16)
    cache_sum = jnp.sum(cache_w.astype(jnp.float32), axis=-1)
    cache_num = jnp.einsum("rgjp,rpgd->rgjd", cache_w, cache_vals, preferred_element_type=jnp.float32)

    my_rows = lax.dynamic_slice_in_dim(row_request[:, 0], my_index * img_local, img_local)
    req_iota = jnp.arange(all_req, dtype=jnp.int32)
    row_slot = jnp.sum(jnp.where(my_rows[:, None] == req_iota[None, :], slot_of_request[None, :], 0), axis=1)
    live = req_iota[:, None] == row_slot[None, :]
    img_k = image_kv[:, :kv_width].reshape(img_local, KVH, HD)
    img_v = image_kv[:, kv_width:].reshape(img_local, KVH, HD)
    qg = all_q.reshape(all_req, KVH, per_group, HD)
    s = jnp.einsum("sgjd,igd->gjsi", qg, img_k, preferred_element_type=jnp.float32) * scale
    masked = jnp.where(live[None, None], s, low_fill)
    img_top = jnp.max(masked, axis=-1)
    own_top = lax.dynamic_update_slice_in_dim(
        jnp.full((KVH, per_group, all_req), low_fill, jnp.float32),
        cache_top.transpose(1, 2, 0), my_index * local_req, 2)
    top = lax.pmax(jnp.maximum(img_top, own_top), "tp")
    w = jnp.where(live[None, None], jnp.exp(s - top[..., None]), 0.0).astype(jnp.bfloat16)
    img_sum = jnp.sum(w.astype(jnp.float32), axis=-1)
    img_num = jnp.einsum("gjsi,igd->sgjd", w, img_v, preferred_element_type=jnp.float32)
    my_top = lax.dynamic_slice_in_dim(top, my_index * local_req, local_req, 2).transpose(2, 0, 1)
    f = jnp.exp(cache_top - my_top)
    num = img_num.at[:].get()
    mine = lax.dynamic_slice_in_dim(num, my_index * local_req, local_req, 0)
    num = lax.dynamic_update_slice_in_dim(num, mine + cache_num * f[..., None], my_index * local_req, 0)
    den = img_sum.transpose(2, 0, 1)
    mine_d = lax.dynamic_slice_in_dim(den, my_index * local_req, local_req, 0)
    den = lax.dynamic_update_slice_in_dim(den, mine_d + cache_sum * f, my_index * local_req, 0)
    num = num.reshape(all_req, QH * HD)
    den = den.reshape(all_req, QH)
    num = lax.psum_scatter(num, "tp", scatter_dimension=1, tiled=True)
    den = lax.psum(den, "tp")
    hpd = QH // tp_size
    den = lax.dynamic_slice_in_dim(den, my_index * hpd, hpd, 1)
    att = (num.reshape(all_req, hpd, HD) / den[:, :, None]).astype(jnp.bfloat16).reshape(all_req, hpd * HD)
    part = jnp.dot(att, out_weight, preferred_element_type=jnp.float32)
    out = lax.psum_scatter(part, "tp", scatter_dimension=0, tiled=True)
    return out.astype(jnp.bfloat16)


def solution(mesh):
    placed = (
        P(("groups", "tp"), None),
        P(("groups", "tp"), None, None),
        P(("groups", "tp")),
        P(("groups", "tp"), None),
        P("groups", None),
        P("groups"),
        P("tp", None),
    )
    return jax.shard_map(
        per_device, mesh=mesh, in_specs=placed, out_specs=P(("groups", "tp"), None), check_vma=False
    )
```

time: 234 us -> 315 us (1.35)
  blocking collectives: 27.4 us -> 119 us
  waiting for transfers between devices: 124 us -> 98 us
  matrix products: 16.6 us -> 32.1 us
  other arithmetic: 4.75 us -> 14.7 us
  starting transfers between devices: 7.79 us -> 0.08 us
    pmax x0 -> x1, blocking collectives: none -> 59.6 us  [per_device(): top = lax.pmax(jnp.maximum(img_top, own_top), 'tp')]
    psum x0 -> x1, blocking collectives: none -> 59 us  [per_device(): den = lax.psum(den, 'tp')]
    all_to_all x1 -> x0, waiting for transfers between devices: 53.3 us -> none  [per_device(): lax.all_to_all(bucket, 'tp', split_axis=0, concat_axis=1, tiled=True)]
    all_to_all x1 -> x0, blocking collectives: 27.4 us -> none  [per_device(): lax.all_to_all(attended, 'tp', split_axis=1, concat_axis=0, tiled=True)]
    dot_general x4, matrix products: 13.7 us -> 29.2 us  [the longest x1 11.9 us: per_device(): jnp.einsum('gjsi,igd->sgjd', w, img_v, preferred_element_type=jnp.float32)]
    all_gather x0 -> x1, waiting for transfers between devices: none -> 14.9 us  [per_device(): all_q = lax.all_gather(queries, 'tp', axis=0, tiled=True)]
    reduce_scatter x1 -> x2, waiting for transfers between devices: 70.3 us -> 82.4 us  [the longest x1 71.6 us: per_device(): out = lax.psum_scatter(part, 'tp', scatter_dimension=0, tiled=True)]
    reduce_sum x5 -> x2, other arithmetic: 1.4 us -> 9.7 us  [the longest x1 9.43 us: per_device(): img_sum = jnp.sum(w.astype(jnp.float32), axis=-1)]
  transfers between devices with their start and end apart: 2 -> 3, of which waited for: 2 -> 3; matrix products, arithmetic and copies ran while one was open for 10% -> 10% of each run, Pallas kernels for 0% -> 0%
where the time goes in v1:
time: 315 us; the launch traced here: 314 us
  blocking collectives  119 us (38%)
  waiting for transfers between devices  98 us (31%)
  local copies, waits for them, and re-layouts  37.6 us (12%)
  matrix products  32.1 us (10%)
  other arithmetic  14.7 us (5%)
  between operations  13.2 us (4%)
    reduce_scatter x1, waiting for transfers between devices, per_device(): out = lax.psum_scatter(part, 'tp', scatter_dimension=0, tiled=True)  71.6 us
    pmax x1, blocking collectives, per_device(): top = lax.pmax(jnp.maximum(img_top, own_top), 'tp')  59.6 us
    psum x1, blocking collectives, per_device(): den = lax.psum(den, 'tp')  59 us
    unnamed x23, local copies, waits for them, and re-layouts  20.1 us
    all_gather x1, waiting for transfers between devices, per_device(): all_q = lax.all_gather(queries, 'tp', axis=0, tiled=True)  14.9 us
    dot_general x1, matrix products, per_device(): jnp.einsum('gjsi,igd->sgjd', w, img_v, preferred_element_type=jnp.float32)  11.9 us
    reduce_scatter x1, waiting for transfers between devices, per_device(): num = lax.psum_scatter(num, 'tp', scatter_dimension=1, tiled=True)  10.8 us
    reduce_sum x1, other arithmetic, per_device(): img_sum = jnp.sum(w.astype(jnp.float32), axis=-1)  9.43 us
  transfers between devices with their start and end apart: 3, of which 3 were waited for; matrix products, arithmetic and copies ran while one was open for 10% of the time, Pallas kernels for 0%

profile of v1, /device:TPU:0, one launch (start us, length us, event | category | flops | bytes accessed | tf_op | source)
XLA Modules:
  0.0 314.3 jit_solution(16774119370258388067)
XLA Ops:
  6.5 0.7 all-gather.2.cloned.1.call-update
  7.3 1.7 fusion.16
  9.0 0.5 copy.106
  9.6 1.3 copy.108
  10.9 6.0 %fusion.15 = (bf16[8,256,1024]{2,1,0:T(8,128)(2,1)}, bf16[8,256,1024]{2,1,0:T(8,128)(2,1)}) fusion(bf16[8,256,2048]{2,1,0:T(8,128)(2,1)} %param.8), kind=kLoop, calls=%fused_computation.31 | loop fusion | bytes 16777216 | tf_op jit(solution)/shard_map/slice | solution.py:29
  16.9 6.5 %copy.109 = bf16[8,256,1024]{1,2,0:T(8,128)(2,1)} copy(bf16[8,256,1024]{2,1,0:T(8,128)(2,1)} %get-tuple-element.7) | data formatting | bytes 8388608
  23.4 6.5 %copy.107 = bf16[8,256,1024]{1,2,0:T(8,128)(2,1)} copy(bf16[8,256,1024]{2,1,0:T(8,128)(2,1)} %get-tuple-element.8) | data formatting | bytes 8388608
  30.0 2.9 select_reduce_fusion
  33.0 0.3 convert_reduce_fusion.1
  33.2 0.7 copy.95
  33.9 0.2 dynamic_update_slice.9
  34.2 0.6 copy-done.4
  34.8 0.2 select_reduce_fusion.1
  35.0 0.1 iota_compare_fusion.1
  35.2 3.5 %fusion.10 = f32[8,8,8,128]{3,2,1,0:T(8,128)S(1)} fusion(bf16[8,256,8,128]{1,3,2,0:T(8,128)(2,1)} %bitcast.56, f32[8,8,8,256]{3,2,1,0:T(8,128)S(1)} %get-tuple-element.14, f32[8,8,8]{2,1,0:T(8,128)S(1)} %get-tuple-element.13, pred[8,256]{1,0:T(8,128)(4,1)S(1)} %iota_compare_fusion.2), kind=kOutput, calls=%fused_computation.24 | convolution fusion | flops 33947648 | bytes 4984832 | tf_op jit(solution)/shard_map/rgjp,rpgd->rgjd/dot_general | solution.py:37
  38.7 14.9 %all-gather.2.cloned.1.call-done = bf16[128,8192]{1,0:T(8,128)(2,1)} async-done(((bf16[8,8192]{1,0:T(8,128)(2,1)}), bf16[128,8192]{1,0:T(8,128)(2,1)}) %all-gather.2.cloned.1.call-update) | async-done | bytes 2097168 | tf_op jit(solution)/shard_map/all_gather | solution.py:25
  53.5 3.2 %copy.80 = bf16[128,8192]{0,1:T(8,128)(2,1)S(1)} copy(bf16[128,8192]{1,0:T(8,128)(2,1)} %all-gather.2.cloned.1.call-done) | data formatting | bytes 4194304 | tf_op jit(solution)/shard_map/all_gather | solution.py:25
  56.8 7.1 %fusion = (f32[8,8,128]{2,1,0:T(8,128)S(1)}, f32[8,512,128,8]{2,1,3,0:T(8,128)}) fusion(pred[128,512]{0,1:T(8,128)(4,1)S(1)} %iota_compare_fusion.1, bf16[512,8,128,1]{0,2,3,1:T(8,128)(2,1)S(1)} %bitcast.60, bf16[128,8,8,128]{0,3,2,1:T(8,128)(2,1)S(1)} %bitcast.59), kind=kOutput, calls=%fused_computation.2 | convolution fusion | flops 1086316544 | bytes 20021248 | tf_op jit(solution)/shard_map/sgjd,igd->gjsi/dot_general | solution.py:46
  63.9 59.6 %pmax.7 = f32[8,8,128]{2,1,0:T(8,128)S(1)} all-reduce(f32[8,8,128]{2,1,0:T(8,128)S(1)} %max.5), channel_id=1, replica_groups=mesh['groups'=2,'tp'=16] {'tp'}, use_global_device_ids=true, to_apply=%region_3.4 | all-reduce | flops 8192 | bytes 65536 | tf_op jit(solution)/shard_map/pmax | solution.py:52
  123.5 9.4 %convert_reduce_fusion = f32[8,8,128]{2,1,0:T(8,128)S(1)} fusion(f32[8,8,128]{2,1,0:T(8,128)S(1)} %pmax.7, f32[8,512,128,8]{2,1,3,0:T(8,128)} %get-tuple-element.12, pred[128,512]{0,1:T(8,128)(4,1)S(1)} %iota_compare_fusion.1), kind=kLoop, calls=%fused_computation.6 | loop fusion | flops 25157632 | bytes 16908288 | tf_op jit(solution)/shard_map/reduce_sum | solution.py:54
  133.0 11.9 %fusion.6 = f32[8,8,128,128]{3,2,1,0:T(8,128)} fusion(bf16[512,8,128,1]{0,2,3,1:T(8,128)(2,1)S(1)} %bitcast.62, f32[8,512,128,8]{2,1,3,0:T(8,128)} %get-tuple-element.12, f32[8,8,128]{2,1,0:T(8,128)S(1)} %pmax.7, pred[128,512]{0,1:T(8,128)(4,1)S(1)} %iota_compare_fusion.1), kind=kOutput, calls=%fused_computation.19 | convolution fusion | flops 1090519040 | bytes 22118400 | tf_op jit(solution)/shard_map/gjsi,igd->sgjd/dot_general | solution.py:55
  144.9 4.6 %copy.118 = f32[128,8,8,128]{3,0,2,1:T(8,128)} copy(f32[128,8,8,128]{3,0,2,1:T(8,128)} %bitcast.61) | data formatting | bytes 8388608
  149.5 0.1 bitcast_add_fusion.1
  149.6 1.9 fusion.5
  151.5 5.3 %copy.94 = f32[128,8,8,128]{0,3,2,1:T(8,128)} copy(f32[128,8,8,128]{3,0,2,1:T(8,128)} %fusion.5) | data formatting | bytes 8388608 | tf_op jit(solution)/shard_map/dynamic_update_slice | solution.py:60
  156.9 0.3 dynamic_update_slice.11
  157.2 59.0 %psum.7 = f32[128,64]{0,1:T(8,128)S(1)} all-reduce(f32[128,64]{0,1:T(8,128)S(1)} %bitcast.65), channel_id=1, replica_groups=mesh['groups'=2,'tp'=16] {'tp'}, use_global_device_ids=true, to_apply=%region_7.8 | all-reduce | flops 8192 | bytes 65536 | tf_op jit(solution)/shard_map/psum | solution.py:67
  216.1 10.8 %reduce-scatter.3.cloned.1.call-done = f32[128,512]{0,1:T(8,128)} async-done(((f32[128,8192]{0,1:T(8,128)}), f32[128,512]{0,1:T(8,128)}) %reduce-scatter.3.cloned.1.call-update) | async-done | bytes 262160 | tf_op jit(solution)/shard_map/reduce_scatter | solution.py:66
  226.9 1.0 fusion.4
  227.9 6.6 %fusion.17 = f32[128,8192]{1,0:T(8,128)} fusion(bf16[128,512]{0,1:T(8,128)(2,1)S(1)} %fusion.4, bf16[512,8192]{1,0:T(8,128)(2,1)} %param.13), kind=kOutput, calls=%fused_computation.33 | convolution fusion | flops 1073741824 | bytes 12713984 | tf_op jit(solution)/shard_map/dot_general | solution.py:71
  234.5 71.6 %reduce-scatter.5.cloned.1.call-done = f32[8,8192]{1,0:T(8,128)} async-done(((f32[128,8192]{1,0:T(8,128)}), f32[8,8192]{1,0:T(8,128)}) %reduce-scatter.5.cloned.1.call-update) | async-done | bytes 262160 | tf_op jit(solution)/shard_map/reduce_scatter | solution.py:72
  306.1 1.6 convert_element_type.24
  (28 shorter events, 0.3 us)
Async XLA Ops:
  6.5 27.6 %copy-start = (s32[8192,1]{0,1:T(1,128)S(1)}, s32[8192,1]{0,1:T(1,128)}, u32[]{:S(2)}) copy-start(s32[8192,1]{0,1:T(1,128)} %param.11) | copy-start | bytes 98308
  6.5 47.0 %all-gather.2.cloned.1.call-start = ((), (), s32[]{:S(2)}) async-start(), calls=%async_computation.2 | async-start | bytes 2228224 | tf_op jit(solution)/shard_map/all_gather | solution.py:25
  7.3 219.6 %reduce-scatter.3.cloned.1.call-start = ((), (), s32[]{:S(2)}) async-start(), calls=%async_computation.3 | async-start | bytes 4456448 | tf_op jit(solution)/shard_map/reduce_scatter | solution.py:66
  16.9 13.0 %copy-start.7 = (s32[8]{0:T(128)S(1)}, s32[8]{0:T(128)}, u32[]{:S(2)}) copy-start(s32[8]{0:T(128)} %param.9) | copy-start | bytes 100
  16.9 13.1 %copy-start.3 = (bf16[8,8192]{1,0:T(8,128)(2,1)S(1)}, bf16[8,8192]{1,0:T(8,128)(2,1)}, u32[]{:S(2)}) copy-start(bf16[8,8192]{1,0:T(8,128)(2,1)} %param.7) | copy-start | bytes 393220
  23.4 11.4 %copy-start.8 = (s32[128]{0:T(128)S(1)}, s32[128]{0:T(128)}, u32[]{:S(2)}) copy-start(s32[128]{0:T(128)} %param.12) | copy-start | bytes 1540
  34.2 0.6 copy-start.4
  56.7 7.2 %copy-start.5 = (f32[8,8,128]{2,1,0:T(8,128)S(1)}, f32[8,8,128]{2,1,0:T(8,128)}, u32[]{:S(2)}) copy-start(f32[8,8,128]{2,1,0:T(8,128)} %copy-done.4) | copy-start | bytes 98308
  123.5 9.4 %copy-start.2 = (bf16[512,1024]{0,1:T(8,128)(2,1)S(1)}, bf16[512,1024]{0,1:T(8,128)(2,1)}, u32[]{:S(2)}) copy-start(bf16[512,1024]{0,1:T(8,128)(2,1)} %copy.108) | copy-start | bytes 3145732
  144.9 4.6 %copy-start.6 = (f32[8,8,8]{0,2,1:T(8,128)S(1)}, f32[8,8,8]{0,2,1:T(8,128)}, u32[]{:S(2)}) copy-start(f32[8,8,8]{0,2,1:T(8,128)} %copy.95) | copy-start | bytes 6148
  156.8 149.3 %reduce-scatter.5.cloned.1.call-start = ((), (), s32[]{:S(2)}) async-start(), calls=%async_computation.4 | async-start | bytes 4456448 | tf_op jit(solution)/shard_map/reduce_scatter | solution.py:72
  226.9 80.9 %copy-start.1 = (s32[8192,1]{0,1:T(1,128)S(1)}, s32[8192,1]{0,1:T(1,128)}, u32[]{:S(2)}) copy-start(s32[8192,1]{0,1:T(1,128)} %param.11) | copy-start | bytes 98308
Sparse Core Ops, SparseCore 0:
  9.5 43.9 all-gather.1
  157.0 69.8 reduce-scatter.2
  234.7 71.4 reduce-scatter.4

commit v2 on v0

--- a/solution.py
+++ b/solution.py
@@ -3,7 +3,10 @@
 import jax
 import jax.numpy as jnp
 from jax import lax
+from jax.experimental import pallas as pl
+from jax.experimental.pallas import tpu as pltpu
 from jax.sharding import PartitionSpec as P
+import functools
 
 QH = 64
 KVH = 8
@@ -20,6 +23,178 @@
     weights = jnp.where(live_mask, jnp.exp(scores - highest[..., None]), 0.0).astype(jnp.bfloat16)
     weight_sums = jnp.sum(weights.astype(jnp.float32), axis=-1)
     return (highest, weights, weight_sums)
+
+
+CHUNKS = 4
+
+
+def bit_of(value, bit):
+    return (value // (1 << bit)) % 2
+
+
+def spread(index, bits):
+    total = 0
+    for r, b in enumerate(bits):
+        total = total + ((index // (1 << r)) % 2) * (1 << b)
+    return total
+
+
+def chunk_orders(n):
+    bits = list(range(n.bit_length() - 1))
+    first = bits
+    second = bits[:1] + bits[2:] + bits[1:2]
+    return [first if c % 2 == 0 else second for c in range(CHUNKS)]
+
+
+def project_kernel(n, att_ref, weight_ref, out_ref, weight, got, acc, sent, landed,
+                   weight_sem, att_send, att_recv, send_sem, recv_sem):
+    me = lax.axis_index("tp")
+    width = out_ref.shape[1] // CHUNKS
+    steps = n.bit_length() - 1
+    orders = chunk_orders(n)
+    loads = []
+    for c in range(CHUNKS):
+        cols = pl.ds(c * width, width)
+        load = pltpu.make_async_copy(weight_ref.at[:, cols], weight.at[:, cols], weight_sem.at[c])
+        load.start()
+        loads.append(load)
+    barrier = pltpu.get_barrier_semaphore()
+
+    @pl.loop(1, n)
+    def _(o):
+        pl.semaphore_signal(barrier, inc=1, device_id={"tp": (me + o) % n}, device_id_type=pl.DeviceIdType.MESH)
+
+    pl.semaphore_wait(barrier, n - 1)
+
+    def att_copy(o):
+        dst = (me + o) % n
+        return pltpu.make_async_remote_copy(
+            src_ref=att_ref.at[dst], dst_ref=got.at[me], send_sem=att_send.at[o], recv_sem=att_recv.at[o],
+            device_id={"tp": dst}, device_id_type=pl.DeviceIdType.MESH)
+
+    @pl.loop(1, n)
+    def _(o):
+        att_copy(o).start()
+
+    got[me] = att_ref[me]
+
+    @pl.loop(1, n)
+    def _(o):
+        src = (me + n - o) % n
+        pltpu.make_async_remote_copy(
+            src_ref=att_ref.at[src], dst_ref=got.at[src], send_sem=att_send.at[o], recv_sem=att_recv.at[o],
+            device_id={"tp": src}, device_id_type=pl.DeviceIdType.MESH).wait_recv()
+
+    rows = got.shape[1]
+    att = got[...].reshape(n * rows, got.shape[2]).astype(jnp.bfloat16)
+
+    def exchange(c, k):
+        m = n >> (k + 1)
+        order = orders[c]
+        wide = width if m > 1 else width // 2
+        half = max(m // 2, 1)
+        first = (n - 2 * m) // 2 if m > 1 else n // 2 - 1
+        where = (pl.ds(first, half), slice(None), pl.ds(c * width, wide))
+        peer = me + (1 - 2 * bit_of(me, order[k])) * (1 << order[k])
+        return pltpu.make_async_remote_copy(
+            src_ref=sent.at[where], dst_ref=landed.at[where], send_sem=send_sem.at[c, k], recv_sem=recv_sem.at[c, k],
+            device_id={"tp": peer}, device_id_type=pl.DeviceIdType.MESH)
+
+    def place(c, k, keep):
+        order = orders[c]
+        base = 0
+        for b in order[:k]:
+            base = base + bit_of(me, b) * (1 << b)
+        own = bit_of(me, order[k])
+        return base + (own if keep else 1 - own) * (1 << order[k]), order[k + 1:]
+
+    def send(c, k):
+        m = n >> (k + 1)
+        base, rest = place(c, k, False)
+        lo = c * width
+        cols = pl.ds(lo, width)
+        if m > 1:
+            first = (n - 2 * m) // 2
+
+            @pl.loop(0, m // 2)
+            def _(p):
+                a = base + spread(2 * p, rest)
+                b = base + spread(2 * p + 1, rest)
+                sent[first + p, :, cols] = jnp.concatenate([acc[a, :, cols], acc[b, :, cols]], axis=0).astype(jnp.bfloat16)
+        else:
+            h = width // 2
+            sent[n // 2 - 1, :, pl.ds(lo, h)] = jnp.concatenate(
+                [acc[base, :, pl.ds(lo, h)], acc[base, :, pl.ds(lo + h, h)]], axis=0).astype(jnp.bfloat16)
+        exchange(c, k).start()
+
+    def receive(c, k):
+        m = n >> (k + 1)
+        exchange(c, k).wait_recv()
+        base, rest = place(c, k, True)
+        lo = c * width
+        cols = pl.ds(lo, width)
+        if m > 1:
+            first = (n - 2 * m) // 2
+
+            @pl.loop(0, m // 2)
+            def _(p):
+                a = base + spread(2 * p, rest)
+                b = base + spread(2 * p + 1, rest)
+                both = landed[first + p, :, cols].astype(jnp.float32)
+                acc[a, :, cols] = acc[a, :, cols] + both[:rows]
+                acc[b, :, cols] = acc[b, :, cols] + both[rows:]
+        else:
+            h = width // 2
+            both = landed[n // 2 - 1, :, pl.ds(lo, h)].astype(jnp.float32)
+            out_ref[:, pl.ds(lo, h)] = (acc[me, :, pl.ds(lo, h)] + both[:rows]).astype(out_ref.dtype)
+            out_ref[:, pl.ds(lo + h, h)] = (acc[me, :, pl.ds(lo + h, h)] + both[rows:]).astype(out_ref.dtype)
+
+    for c in range(CHUNKS):
+        loads[c].wait()
+        cols = pl.ds(c * width, width)
+        acc[:, :, cols] = jnp.dot(att, weight[:, cols], preferred_element_type=jnp.float32).reshape(n, rows, width)
+        send(c, 0)
+    for k in range(steps):
+        for c in range(CHUNKS):
+            receive(c, k)
+            if k + 1 < steps:
+                send(c, k + 1)
+
+    @pl.loop(1, n)
+    def _(o):
+        att_copy(o).wait_send()
+
+    for k in range(steps):
+        for c in range(CHUNKS):
+            exchange(c, k).wait_send()
+
+
+def project(attended, out_weight, n):
+    rows = attended.shape[0]
+    model = out_weight.shape[1]
+    depth = out_weight.shape[0]
+    steps = n.bit_length() - 1
+    by_owner = jnp.transpose(attended.reshape(rows, n, depth), (1, 0, 2))
+    return pl.pallas_call(
+        functools.partial(project_kernel, n),
+        out_shape=jax.ShapeDtypeStruct((rows, model), jnp.bfloat16),
+        in_specs=[pl.BlockSpec(memory_space=pltpu.VMEM), pl.BlockSpec(memory_space=pl.ANY)],
+        out_specs=pl.BlockSpec(memory_space=pltpu.VMEM),
+        scratch_shapes=[
+            pltpu.VMEM((depth, model), jnp.bfloat16),
+            pltpu.VMEM((n, rows, depth), jnp.float32),
+            pltpu.VMEM((n, rows, model), jnp.float32),
+            pltpu.VMEM((n // 2, 2 * rows, model), jnp.bfloat16),
+            pltpu.VMEM((n // 2, 2 * rows, model), jnp.bfloat16),
+            pltpu.SemaphoreType.DMA((CHUNKS,)),
+            pltpu.SemaphoreType.DMA((n,)),
+            pltpu.SemaphoreType.DMA((n,)),
+            pltpu.SemaphoreType.DMA((CHUNKS, steps)),
+            pltpu.SemaphoreType.DMA((CHUNKS, steps)),
+        ],
+        compiler_params=pltpu.CompilerParams(
+            collective_id=0, has_side_effects=True, vmem_limit_bytes=48 * 1024 * 1024),
+    )(by_owner, out_weight)
 
 
 def per_device(queries, cache_kv, cache_len, image_kv, row_request, slot_of_request, out_weight):
@@ -81,15 +256,7 @@
     attended = (cache_num * factor[..., None] + image_num) / (cache_sum * factor + image_sum)[
         ..., None
     ]
-    attended = attended.reshape(local_req, QH * HD).astype(jnp.bfloat16)
-    by_head = lax.all_to_all(attended, "tp", split_axis=1, concat_axis=0, tiled=True)
-    summed = lax.psum_scatter(
-        jnp.dot(by_head, out_weight, preferred_element_type=jnp.float32),
-        "tp",
-        scatter_dimension=0,
-        tiled=True,
-    )
-    return summed.astype(jnp.bfloat16)
+    return project(attended.reshape(local_req, QH * HD), out_weight, tp_size)
 
 
 def solution(mesh):

time: 234 us -> 162 us (0.69)
  waiting for transfers between devices: 124 us -> 53.5 us
  Pallas kernels: 0 us -> 46.2 us
  blocking collectives: 27.4 us -> 0 us
  between operations: 13.5 us -> 0.14 us
  matrix products: 16.6 us -> 9.9 us
    reduce_scatter x1 -> x0, waiting for transfers between devices: 70.3 us -> none  [per_device(): lax.psum_scatter(jnp.dot(by_head, out_weight, preferred_element_type=jnp....]
    pallas_call x0 -> x1, Pallas kernels: none -> 46.2 us  [project(): pl.pallas_call(functools.partial(project_kernel, n), out_shape=jax.ShapeD...]
    all_to_all x1 -> x0, blocking collectives: 27.4 us -> none  [per_device(): lax.all_to_all(attended, 'tp', split_axis=1, concat_axis=0, tiled=True)]
    dot_general x1 -> x0, matrix products: 6.69 us -> none  [per_device(): jnp.dot(by_head, out_weight, preferred_element_type=jnp.float32)]
    unnamed x11 -> x12, local copies, waits for them, and re-layouts: 13.5 us -> 14.1 us
  transfers between devices with their start and end apart: 2 -> 1, of which waited for: 2 -> 1; matrix products, arithmetic and copies ran while one was open for 10% -> 15% of each run, Pallas kernels for 0% -> 0%
where the time goes in v2:
time: 162 us; the launch traced here: 161 us
  waiting for transfers between devices  53.5 us (33%)
  Pallas kernels  46.2 us (29%)
  local copies, waits for them, and re-layouts  40.4 us (25%)
  matrix products  9.9 us (6%)
  starting transfers between devices  7.58 us (5%)
  other arithmetic  3.13 us (2%)
    all_to_all x1, waiting for transfers between devices, per_device(): lax.all_to_all(bucket, 'tp', split_axis=0, concat_axis=1, tiled=True)  53.5 us
    pallas_call x1, Pallas kernels, project(): pl.pallas_call(functools.partial(project_kernel, n), out_shape=jax.ShapeD...  46.2 us
    unnamed x12, local copies, waits for them, and re-layouts  14.1 us
    all_to_all x1, starting transfers between devices, per_device(): lax.all_to_all(bucket, 'tp', split_axis=0, concat_axis=1, tiled=True)  7.58 us
    scatter x1, local copies, waits for them, and re-layouts, per_device(): bucket = bucket.at[row_slot * capacity + row_rank].set(image_kv)  7.26 us
    slice x1, local copies, waits for them, and re-layouts, per_device(): cache_keys = cache_kv[:, :, :kv_width].reshape(local_req, CACHE, KVH, HD)  5.93 us
    slice x2, local copies, waits for them, and re-layouts, per_device(): arrived[:, :, kv_width:].reshape(local_req, tp_size * capacity, KVH, HD)  5.46 us
    slice x1, local copies, waits for them, and re-layouts, per_device(): arrived[:, :, :kv_width].reshape(local_req, tp_size * capacity, KVH, HD)  3.93 us
  transfers between devices with their start and end apart: 1, of which 1 were waited for; matrix products, arithmetic and copies ran while one was open for 15% of the time, Pallas kernels for 0%

profile of v2, /device:TPU:0, one launch (start us, length us, event | category | flops | bytes accessed | tf_op | source)
XLA Modules:
  0.0 160.9 jit_solution(13982702220286994927)
XLA Ops:
  0.0 0.7 constant_dynamic-slice_fusion
  0.7 0.3 convert_reduce_fusion
  0.9 0.9 select_reduce_fusion.2
  1.9 7.3 %scatter_custom_fusion = bf16[1024,2048]{1,0:T(8,128)(2,1)} fusion(s32[512]{0:T(512)S(1)} %bitcast.40, bf16[512,2048]{1,0:T(8,128)(2,1)} %param.10, bf16[]{:T(256)} %constant.4.clone.1), kind=kCustom, calls=%fused_computation.2 | custom fusion | bytes 4194816 | tf_op jit(solution)/shard_map/scatter | solution.py:218
  9.1 7.6 %all-to-all-start = ((bf16[128,8,2048]{2,1,0:T(8,128)(2,1)}), bf16[128,8,2048]{2,1,0:T(8,128)(2,1)}, u32[]{:S(2)}, u32[]{:S(2)}) async-start(bf16[128,8,2048]{2,1,0:T(8,128)(2,1)} %bitcast.28), calls=%async_computation | async-start | bytes 8388608 | tf_op jit(solution)/shard_map/all_to_all | solution.py:220
  16.7 0.1 lt.76
  16.8 0.5 broadcast.79
  17.3 0.7 reduce.5
  18.1 0.2 select_reduce_fusion.3
  18.3 0.4 convert_reduce_fusion.3
  18.7 0.1 copy.38
  18.8 0.1 lt.79
  18.8 0.1 lt.80
  18.9 5.9 %fusion.9 = (bf16[8,256,1024]{2,1,0:T(8,128)(2,1)}, bf16[8,256,1024]{2,1,0:T(8,128)(2,1)}) fusion(bf16[8,256,2048]{2,1,0:T(8,128)(2,1)} %param.8), kind=kLoop, calls=%fused_computation.37 | loop fusion | bytes 16777216 | tf_op jit(solution)/shard_map/slice | solution.py:222
  24.9 6.4 %copy.50 = bf16[8,256,1024]{1,2,0:T(8,128)(2,1)} copy(bf16[8,256,1024]{2,1,0:T(8,128)(2,1)} %get-tuple-element.7) | data formatting | bytes 8388608
  31.3 6.5 %copy.51 = bf16[8,256,1024]{1,2,0:T(8,128)(2,1)} copy(bf16[8,256,1024]{2,1,0:T(8,128)(2,1)} %get-tuple-element.8) | data formatting | bytes 8388608
  37.8 0.1 iota_compare_fusion.2
  37.9 2.9 %select_reduce_fusion = (f32[8,8,8]{2,1,0:T(8,128)S(1)}, f32[8,8,8,256]{3,2,1,0:T(8,128)S(1)}) fusion(pred[8,256]{1,0:T(8,128)(4,1)S(1)} %iota_compare_fusion.2, bf16[8,256,8,128]{1,3,2,0:T(8,128)(2,1)} %bitcast.30, bf16[8,8,8,128]{3,0,2,1:T(8,128)(2,1)S(1)} %bitcast.34), kind=kOutput, calls=%fused_computation.14 | convolution fusion | flops 33947136 | bytes 4853760 | tf_op jit(solution)/shard_map/rgjd,rpgd->rgjp/dot_general | solution.py:225
  40.8 53.5 %all-to-all-done = bf16[128,8,2048]{2,1,0:T(8,128)(2,1)} async-done(((bf16[128,8,2048]{2,1,0:T(8,128)(2,1)}), bf16[128,8,2048]{2,1,0:T(8,128)(2,1)}, u32[]{:S(2)}, u32[]{:S(2)}) %all-to-all-start) | async-done | bytes 4194336 | tf_op jit(solution)/shard_map/all_to_all | solution.py:220
  94.4 2.5 %copy.62 = bf16[8,16,8,2048]{3,2,1,0:T(8,128)(2,1)S(1)} copy(bf16[8,16,8,2048]{3,2,0,1:T(8,128)(2,1)} %bitcast.9) | data formatting | bytes 8388608 | tf_op jit(solution)/shard_map/all_to_all | solution.py:220
  96.9 2.4 %fusion.10 = (bf16[8,128,1024]{2,1,0:T(8,128)(2,1)}, bf16[8,128,1024]{2,1,0:T(8,128)(2,1)}) fusion(bf16[8,128,2048]{2,1,0:T(8,128)(2,1)S(1)} %bitcast.31), kind=kLoop, calls=%fused_computation.38 | loop fusion | bytes 8388608 | tf_op jit(solution)/shard_map/slice | solution.py:246
  99.3 3.0 %copy.43 = bf16[8,128,1024]{1,2,0:T(8,128)(2,1)S(1)} copy(bf16[8,128,1024]{2,1,0:T(8,128)(2,1)} %get-tuple-element.9) | data formatting | bytes 4194304 | tf_op jit(solution)/shard_map/slice | solution.py:246
  102.3 3.9 %copy.40 = bf16[8,128,1024]{1,2,0:T(8,128)(2,1)} copy(bf16[8,128,1024]{2,1,0:T(8,128)(2,1)} %get-tuple-element.10) | data formatting | bytes 4194304 | tf_op jit(solution)/shard_map/slice | solution.py:245
  106.3 2.3 %select_reduce_fusion.1 = (f32[8,8,8]{2,1,0:T(8,128)S(1)}, f32[8,8,128,8]{2,3,1,0:T(8,128)S(1)}) fusion(pred[8,128]{1,0:T(8,128)(4,1)S(1)} %broadcast_compare_fusion, bf16[8,128,8,128]{1,3,2,0:T(8,128)(2,1)} %bitcast.33, bf16[8,8,8,128]{3,0,2,1:T(8,128)(2,1)S(1)} %bitcast.35), kind=kOutput, calls=%fused_computation.18 | convolution fusion | flops 16973312 | bytes 2493440 | tf_op jit(solution)/shard_map/rgjd,rsgd->rgjs/dot_general | solution.py:248
  108.6 0.3 convert_reduce_fusion.1
  108.9 0.3 convert_reduce_fusion.2
  109.2 3.4 %convolution_multiply_fusion.2 = f32[8,8,8,128]{3,2,1,0:T(8,128)S(1)} fusion(bf16[8,256,8,128]{1,3,2,0:T(8,128)(2,1)} %bitcast.29, f32[8,8,8]{2,1,0:T(8,128)S(1)} %get-tuple-element.6, f32[8,8,8,256]{3,2,1,0:T(8,128)S(1)} %get-tuple-element.14, f32[8,8,8]{2,1,0:T(8,128)S(1)} %get-tuple-element.11, pred[8,256]{1,0:T(8,128)(4,1)S(1)} %iota_compare_fusion.2), kind=kOutput, calls=%fused_computation.8 | convolution fusion | flops 34013184 | bytes 4986880 | tf_op jit(solution)/shard_map/rgjp,rpgd->rgjd/dot_general | solution.py:232
  112.6 1.2 fusion.2
  113.8 0.1 reshape_reshape.3
  113.9 0.2 copy.63
  114.1 46.2 %shard_map.73 = bf16[8,8192]{1,0:T(8,128)(2,1)S(1)} custom-call(f32[16,8,512]{2,1,0:T(8,128)S(1)} %bitcast.27, bf16[512,8192]{1,0:T(8,128)(2,1)} %weight_ref.1), custom_call_target="tpu_custom_call" | custom-call | tf_op jit(solution)/shard_map/pallas_call | solution.py:178
  160.2 0.7 copy.65
  (16 shorter events, 0.1 us)
Async XLA Ops:
  9.1 8.2 %copy-start.1 = (s32[8192,1]{0,1:T(1,128)S(1)}, s32[8192,1]{0,1:T(1,128)}, u32[]{:S(2)}) copy-start(s32[8192,1]{0,1:T(1,128)} %param.11) | copy-start | bytes 98308
  9.1 9.0 %copy-start.2 = (s32[128]{0:T(128)S(1)}, s32[128]{0:T(128)}, u32[]{:S(2)}) copy-start(s32[128]{0:T(128)} %param.12) | copy-start | bytes 1540
  9.1 85.3 %all-to-all-start = ((bf16[128,8,2048]{2,1,0:T(8,128)(2,1)}), bf16[128,8,2048]{2,1,0:T(8,128)(2,1)}, u32[]{:S(2)}, u32[]{:S(2)}) async-start(bf16[128,8,2048]{2,1,0:T(8,128)(2,1)} %bitcast.28), calls=%async_computation | async-start | bytes 8388608 | tf_op jit(solution)/shard_map/all_to_all | solution.py:220
  31.3 6.5 %copy-start.3 = (s32[8]{0:T(128)S(1)}, s32[8]{0:T(128)}, u32[]{:S(2)}) copy-start(s32[8]{0:T(128)} %param.9) | copy-start | bytes 100
  31.3 6.6 %copy-start = (bf16[8,8192]{1,0:T(8,128)(2,1)S(1)}, bf16[8,8192]{1,0:T(8,128)(2,1)}, u32[]{:S(2)}) copy-start(bf16[8,8192]{1,0:T(8,128)(2,1)} %param.7) | copy-start | bytes 393220

commit v3 on v2

--- a/solution.py
+++ b/solution.py
@@ -46,8 +46,103 @@
     return [first if c % 2 == 0 else second for c in range(CHUNKS)]
 
 
-def project_kernel(n, att_ref, weight_ref, out_ref, weight, got, acc, sent, landed,
-                   weight_sem, att_send, att_recv, send_sem, recv_sem):
+def image_heads(n, query_ref, image_ref, bias_ref, num, stat):
+    per_dev = QH // n
+    per_chunk = per_dev // 2
+    per_group = QH // KVH
+    stat[...] = jnp.zeros_like(stat)
+
+    @pl.loop(0, KVH)
+    def _(g):
+        keys = image_ref[:, pl.ds(pl.multiple_of(g * HD, HD), HD)]
+        vals = image_ref[:, pl.ds(pl.multiple_of((KVH + g) * HD, HD), HD)].T
+        for j in range(per_group):
+            q = query_ref[:, pl.ds(pl.multiple_of((g * per_group + j) * HD, HD), HD)]
+            s = lax.dot_general(keys, q, (((1,), (1,)), ((), ())), preferred_element_type=jnp.float32)
+            s = s * (1.0 / math.sqrt(HD)) + bias_ref[...]
+            top = jnp.maximum(jnp.max(s, axis=0, keepdims=True), 0.1 * low_fill)
+            w = jnp.exp(s - top).astype(jnp.bfloat16)
+            dst = g * (per_group // per_dev) + j // per_dev
+            c, i = (j % per_dev) // per_chunk, j % per_chunk
+            num[c, dst, pl.ds(i * HD, HD), :] = jnp.dot(vals, w, preferred_element_type=jnp.float32)
+            stat[c, dst, pl.ds(i, 1), :] = top
+            stat[c, dst, pl.ds(4 + i, 1), :] = jnp.sum(w.astype(jnp.float32), axis=0, keepdims=True)
+
+
+def sum_heads(n, num, stat, num_sent, num_got, stat_sent, stat_got, send_sem, recv_sem):
+    me = lax.axis_index("tp")
+    steps = n.bit_length() - 1
+    per_chunk = QH // n // 2
+
+    def copies(c, k):
+        m = n >> (k + 1)
+        order = chunk_orders(n)[c]
+        peer = me + (1 - 2 * bit_of(me, order[k])) * (1 << order[k])
+        at = pl.ds(n - 2 * m, m)
+        return [pltpu.make_async_remote_copy(
+            src_ref=a.at[c, at], dst_ref=b.at[c, at], send_sem=send_sem.at[c, k, i], recv_sem=recv_sem.at[c, k, i],
+            device_id={"tp": peer}, device_id_type=pl.DeviceIdType.MESH)
+            for i, (a, b) in enumerate([(stat_sent, stat_got), (num_sent, num_got)])]
+
+    def place(c, k, keep):
+        order = chunk_orders(n)[c]
+        base = 0
+        for b in order[:k]:
+            base = base + bit_of(me, b) * (1 << b)
+        own = bit_of(me, order[k])
+        return base + (own if keep else 1 - own) * (1 << order[k]), order[k + 1:]
+
+    def send(c, k):
+        m = n >> (k + 1)
+        base, rest = place(c, k, False)
+
+        @pl.loop(0, m)
+        def _(p):
+            d = base + spread(p, rest)
+            num_sent[c, n - 2 * m + p] = num[c, d].astype(jnp.bfloat16)
+            stat_sent[c, n - 2 * m + p] = stat[c, d]
+
+        for copy in copies(c, k):
+            copy.start()
+
+    def receive(c, k):
+        m = n >> (k + 1)
+        base, rest = place(c, k, True)
+        for copy in copies(c, k):
+            copy.wait_recv()
+
+        @pl.loop(0, m)
+        def _(p):
+            d = base + spread(p, rest)
+            for i in range(per_chunk):
+                ta, tb = stat[c, d, pl.ds(i, 1), :], stat_got[c, n - 2 * m + p, pl.ds(i, 1), :]
+                sa, sb = stat[c, d, pl.ds(4 + i, 1), :], stat_got[c, n - 2 * m + p, pl.ds(4 + i, 1), :]
+                top = jnp.maximum(ta, tb)
+                ea, eb = jnp.exp(ta - top), jnp.exp(tb - top)
+                part = pl.ds(i * HD, HD)
+                other = num_got[c, n - 2 * m + p, part, :].astype(jnp.float32)
+                num[c, d, part, :] = num[c, d, part, :] * ea + other * eb
+                stat[c, d, pl.ds(i, 1), :] = top
+                stat[c, d, pl.ds(4 + i, 1), :] = sa * ea + sb * eb
+
+    for c in range(2):
+        send(c, 0)
+    for k in range(steps):
+        for c in range(2):
+            receive(c, k)
+            if k + 1 < steps:
+                send(c, k + 1)
+    return [copy for k in range(steps) for c in range(2) for copy in copies(c, k)]
+
+
+def project_kernel(n, fused, *refs):
+    if fused:
+        (att_ref, weight_ref, query_ref, image_ref, bias_ref, out_ref, weight, got, acc, sent, landed,
+         weight_sem, att_send, att_recv, send_sem, recv_sem,
+         num, stat, num_sent, num_got, stat_sent, stat_got, head_send, head_recv) = refs
+    else:
+        (att_ref, weight_ref, out_ref, weight, got, acc, sent, landed,
+         weight_sem, att_send, att_recv, send_sem, recv_sem) = refs
     me = lax.axis_index("tp")
     width = out_ref.shape[1] // CHUNKS
     steps = n.bit_length() - 1
@@ -77,6 +172,10 @@
         att_copy(o).start()
 
     got[me] = att_ref[me]
+    started = []
+    if fused:
+        image_heads(n, query_ref, image_ref, bias_ref, num, stat)
+        started = sum_heads(n, num, stat, num_sent, num_got, stat_sent, stat_got, head_send, head_recv)
 
     @pl.loop(1, n)
     def _(o):
@@ -86,7 +185,22 @@
             device_id={"tp": src}, device_id_type=pl.DeviceIdType.MESH).wait_recv()
 
     rows = got.shape[1]
-    att = got[...].reshape(n * rows, got.shape[2]).astype(jnp.bfloat16)
+    if fused:
+        per_dev = QH // n
+        cached = got[...].reshape(n * rows, got.shape[2]).T
+        depth = per_dev * HD
+        pieces = []
+        for h in range(per_dev):
+            c, i = h // (per_dev // 2), h % (per_dev // 2)
+            ct, cs = cached[depth + h:depth + h + 1], cached[depth + 64 + h:depth + 65 + h]
+            it, isum = stat[c, me, pl.ds(i, 1), :], stat[c, me, pl.ds(4 + i, 1), :]
+            top = jnp.maximum(ct, it)
+            ce, ie = jnp.exp(ct - top), jnp.exp(it - top)
+            total = cached[h * HD:(h + 1) * HD] * ce + num[c, me, pl.ds(i * HD, HD), :] * ie
+            pieces.append((total / (cs * ce + isum * ie)).T)
+        att = jnp.concatenate(pieces, axis=1).astype(jnp.bfloat16)
+    else:
+        att = got[...].reshape(n * rows, got.shape[2]).astype(jnp.bfloat16)
 
     def exchange(c, k):
         m = n >> (k + 1)
@@ -164,25 +278,41 @@
     def _(o):
         att_copy(o).wait_send()
 
+    for copy in started:
+        copy.wait_send()
     for k in range(steps):
         for c in range(CHUNKS):
             exchange(c, k).wait_send()
 
 
-def project(attended, out_weight, n):
-    rows = attended.shape[0]
+def project(by_owner, out_weight, n, image=()):
+    rows = by_owner.shape[1]
     model = out_weight.shape[1]
     depth = out_weight.shape[0]
     steps = n.bit_length() - 1
-    by_owner = jnp.transpose(attended.reshape(rows, n, depth), (1, 0, 2))
+    extra = []
+    if image:
+        half = depth // 2
+        every = n * rows
+        extra = [
+            pltpu.VMEM((2, n, half, every), jnp.float32),
+            pltpu.VMEM((2, n, 8, every), jnp.float32),
+            pltpu.VMEM((2, n - 1, half, every), jnp.bfloat16),
+            pltpu.VMEM((2, n - 1, half, every), jnp.bfloat16),
+            pltpu.VMEM((2, n - 1, 8, every), jnp.float32),
+            pltpu.VMEM((2, n - 1, 8, every), jnp.float32),
+            pltpu.SemaphoreType.DMA((2, steps, 2)),
+            pltpu.SemaphoreType.DMA((2, steps, 2)),
+        ]
     return pl.pallas_call(
-        functools.partial(project_kernel, n),
+        functools.partial(project_kernel, n, bool(image)),
         out_shape=jax.ShapeDtypeStruct((rows, model), jnp.bfloat16),
-        in_specs=[pl.BlockSpec(memory_space=pltpu.VMEM), pl.BlockSpec(memory_space=pl.ANY)],
+        in_specs=[pl.BlockSpec(memory_space=pltpu.VMEM), pl.BlockSpec(memory_space=pl.ANY)]
+        + [pl.BlockSpec(memory_space=pltpu.VMEM)] * len(image),
         out_specs=pl.BlockSpec(memory_space=pltpu.VMEM),
         scratch_shapes=[
             pltpu.VMEM((depth, model), jnp.bfloat16),
-            pltpu.VMEM((n, rows, depth), jnp.float32),
+            pltpu.VMEM(by_owner.shape, jnp.float32),
             pltpu.VMEM((n, rows, model), jnp.float32),
             pltpu.VMEM((n // 2, 2 * rows, model), jnp.bfloat16),
             pltpu.VMEM((n // 2, 2 * rows, model), jnp.bfloat16),
@@ -191,10 +321,10 @@
             pltpu.SemaphoreType.DMA((n,)),
             pltpu.SemaphoreType.DMA((CHUNKS, steps)),
             pltpu.SemaphoreType.DMA((CHUNKS, steps)),
-        ],
+        ] + extra,
         compiler_params=pltpu.CompilerParams(
             collective_id=0, has_side_effects=True, vmem_limit_bytes=48 * 1024 * 1024),
-    )(by_owner, out_weight)
+    )(by_owner, out_weight, *image)
 
 
 def per_device(queries, cache_kv, cache_len, image_kv, row_request, slot_of_request, out_weight):
@@ -211,6 +341,33 @@
     row_slot = jnp.sum(
         jnp.where(my_rows[:, None] == req_iota[None, :], slot_of_request[None, :], 0), axis=1
     )
+    grouped = queries.reshape(local_req, KVH, QH // KVH, HD)
+    cache_keys = cache_kv[:, :, :kv_width].reshape(local_req, CACHE, KVH, HD)
+    cache_vals = cache_kv[:, :, kv_width:].reshape(local_req, CACHE, KVH, HD)
+    cache_scores = (
+        jnp.einsum("rgjd,rpgd->rgjp", grouped, cache_keys, preferred_element_type=jnp.float32)
+        * score_scale
+    )
+    cache_live = (jnp.arange(CACHE, dtype=jnp.int32)[None, :] < cache_len[:, None])[
+        :, None, None, :
+    ]
+    cache_top, cache_weights, cache_sum = softmax_part(cache_scores, cache_live, low_fill)
+    cache_num = jnp.einsum(
+        "rgjp,rpgd->rgjd", cache_weights, cache_vals, preferred_element_type=jnp.float32
+    )
+    per_dev = QH // tp_size
+    if per_dev % 2 == 0 and per_dev <= QH // KVH:
+        live = row_slot[:, None] == req_iota[None, :]
+        bias = jnp.where(live, 0.0, low_fill).astype(jnp.float32)
+        every = lax.all_gather(queries, "tp", axis=0, tiled=True)
+
+        def spare(x):
+            x = x.reshape(local_req, tp_size, per_dev)
+            return jnp.pad(x, ((0, 0), (0, 0), (0, 64 - per_dev)))
+
+        packed = jnp.concatenate(
+            [cache_num.reshape(local_req, tp_size, per_dev * HD), spare(cache_top), spare(cache_sum)], axis=2)
+        return project(jnp.transpose(packed, (1, 0, 2)), out_weight, tp_size, (every, image_kv, bias))
     row_iota = jnp.arange(img_local, dtype=jnp.int32)
     earlier = (my_rows[:, None] == my_rows[None, :]) & (row_iota[None, :] < row_iota[:, None])
     row_rank = jnp.sum(earlier.astype(jnp.int32), axis=1)
@@ -218,20 +375,6 @@
     bucket = bucket.at[row_slot * capacity + row_rank].set(image_kv)
     bucket = bucket.reshape(all_req, capacity, 2 * kv_width)
     arrived = lax.all_to_all(bucket, "tp", split_axis=0, concat_axis=1, tiled=True)
-    grouped = queries.reshape(local_req, KVH, QH // KVH, HD)
-    cache_keys = cache_kv[:, :, :kv_width].reshape(local_req, CACHE, KVH, HD)
-    cache_vals = cache_kv[:, :, kv_width:].reshape(local_req, CACHE, KVH, HD)
-    cache_scores = (
-        jnp.einsum("rgjd,rpgd->rgjp", grouped, cache_keys, preferred_element_type=jnp.float32)
-        * score_scale
-    )
-    cache_live = (jnp.arange(CACHE, dtype=jnp.int32)[None, :] < cache_len[:, None])[
-        :, None, None, :
-    ]
-    cache_top, cache_weights, cache_sum = softmax_part(cache_scores, cache_live, low_fill)
-    cache_num = jnp.einsum(
-        "rgjp,rpgd->rgjd", cache_weights, cache_vals, preferred_element_type=jnp.float32
-    )
     my_slots = my_index * local_req + jnp.arange(local_req, dtype=jnp.int32)
     owned_slot = slot_of_request[:, None] == my_slots[None, :]
     my_requests = jnp.sum(jnp.where(owned_slot, req_iota[:, None], 0), axis=0)
@@ -256,7 +399,8 @@
     attended = (cache_num * factor[..., None] + image_num) / (cache_sum * factor + image_sum)[
         ..., None
     ]
-    return project(attended.reshape(local_req, QH * HD), out_weight, tp_size)
+    by_owner = jnp.transpose(attended.reshape(local_req, tp_size, QH * HD // tp_size), (1, 0, 2))
+    return project(by_owner, out_weight, tp_size)
 
 
 def solution(mesh):

time: 162 us -> 122 us (0.75)
  waiting for transfers between devices: 53.5 us -> 20 us
  local copies, waits for them, and re-layouts: 40.4 us -> 22 us
  between operations: 0.14 us -> 13.4 us
  Pallas kernels: 46.2 us -> 58.9 us
  starting transfers between devices: 7.58 us -> 0.01 us
  matrix products: 9.9 us -> 6.48 us
  other arithmetic: 3.13 us -> 0.8 us
    all_to_all x1 -> x0, waiting for transfers between devices: 53.5 us -> none  [per_device(): lax.all_to_all(bucket, 'tp', split_axis=0, concat_axis=1, tiled=True)]
    all_gather x0 -> x1, waiting for transfers between devices: none -> 19.3 us  [per_device(): every = lax.all_gather(queries, 'tp', axis=0, tiled=True)]
    pallas_call x1, Pallas kernels: 46.2 us -> 58.9 us  [project(): pl.pallas_call(functools.partial(project_kernel, n, bool(image)), out_sha...]
    slice x4 -> x1, local copies, waits for them, and re-layouts: 15.3 us -> 5.97 us  [per_device(): cache_vals = cache_kv[:, :, kv_width:].reshape(local_req, CACHE, KVH, HD)]
    all_to_all x1 -> x0, starting transfers between devices: 7.58 us -> none  [per_device(): lax.all_to_all(bucket, 'tp', split_axis=0, concat_axis=1, tiled=True)]
    scatter x1 -> x0, local copies, waits for them, and re-layouts: 7.26 us -> none  [per_device(): bucket = bucket.at[row_slot * capacity + row_rank].set(image_kv)]
    dot_general x2 -> x0, matrix products: 3.56 us -> none  [the longest x1 2.32 us: per_device(): jnp.einsum('rgjd,rsgd->rgjs', grouped, image_keys, preferred_element_type...]
    all_to_all x1 -> x0, local copies, waits for them, and re-layouts: 2.5 us -> none  [per_device(): lax.all_to_all(bucket, 'tp', split_axis=0, concat_axis=1, tiled=True)]
  transfers between devices with their start and end apart: 1 -> 1, of which waited for: 1 -> 1; matrix products, arithmetic and copies ran while one was open for 15% -> 22% of each run, Pallas kernels for 0% -> 0%
where the time goes in v3:
time: 122 us
  Pallas kernels  58.9 us (48%)
  local copies, waits for them, and re-layouts  22 us (18%)
  waiting for transfers between devices  20 us (16%)
  between operations  13.4 us (11%)
  matrix products  6.48 us (5%)
    pallas_call x1, Pallas kernels, project(): pl.pallas_call(functools.partial(project_kernel, n, bool(image)), out_sha...  58.9 us
    all_gather x1, waiting for transfers between devices, per_device(): every = lax.all_gather(queries, 'tp', axis=0, tiled=True)  19.3 us
    unnamed x15, local copies, waits for them, and re-layouts  15.3 us
    slice x1, local copies, waits for them, and re-layouts, per_device(): cache_vals = cache_kv[:, :, kv_width:].reshape(local_req, CACHE, KVH, HD)  5.97 us
    dot_general x1, matrix products, per_device(): jnp.einsum('rgjp,rpgd->rgjd', cache_weights, cache_vals, preferred_elemen...  3.56 us
    dot_general x1, matrix products, per_device(): jnp.einsum('rgjd,rpgd->rgjp', grouped, cache_keys, preferred_element_type...  2.92 us
  transfers between devices with their start and end apart: 1, of which 1 were waited for; matrix products, arithmetic and copies ran while one was open for 22% of the time, Pallas kernels for 0%

profile of v3, /device:TPU:0, one launch (start us, length us, event | category | flops | bytes accessed | tf_op | source)
XLA Modules:
  0.0 121.6 jit_solution(14950942801688502847)
XLA Ops:
  6.5 0.0 copy-start
  6.5 0.0 all-gather.2.cloned.1.call-start
  6.5 0.7 all-gather.2.cloned.1.call-update
  7.3 6.0 %fusion.6 = (bf16[8,256,1024]{2,1,0:T(8,128)(2,1)}, bf16[8,256,1024]{2,1,0:T(8,128)(2,1)}) fusion(bf16[8,256,2048]{2,1,0:T(8,128)(2,1)} %param.8), kind=kLoop, calls=%fused_computation.21 | loop fusion | bytes 16777216 | tf_op jit(solution)/shard_map/slice | solution.py:346
  13.2 6.5 %copy.40 = bf16[8,256,1024]{1,2,0:T(8,128)(2,1)} copy(bf16[8,256,1024]{2,1,0:T(8,128)(2,1)} %get-tuple-element.6) | data formatting | bytes 8388608
  19.7 0.0 copy-start.4
  19.7 0.0 copy-start.3
  19.7 6.6 %copy.41 = bf16[8,256,1024]{1,2,0:T(8,128)(2,1)} copy(bf16[8,256,1024]{2,1,0:T(8,128)(2,1)} %get-tuple-element.5) | data formatting | bytes 8388608
  26.3 0.0 copy-done.4
  26.3 0.1 iota_compare_fusion.5
  26.4 0.0 copy-done.3
  26.4 2.9 %select_reduce_fusion = (f32[8,8,8]{2,1,0:T(8,128)S(1)}, f32[8,8,8,256]{3,2,1,0:T(8,128)S(1)}) fusion(pred[8,256]{1,0:T(8,128)(4,1)S(1)} %iota_compare_fusion.5, bf16[8,256,8,128]{1,3,2,0:T(8,128)(2,1)} %bitcast.13, bf16[8,8,8,128]{3,0,2,1:T(8,128)(2,1)S(1)} %bitcast.14), kind=kOutput, calls=%fused_computation.3 | convolution fusion | flops 33947136 | bytes 4853760 | tf_op jit(solution)/shard_map/rgjd,rpgd->rgjp/dot_general | solution.py:348
  29.3 0.0 copy-start.5
  29.3 0.0 copy-start.1
  29.3 0.1 copy.33
  29.4 3.6 %fusion.4 = f32[8,8,8,128]{3,2,1,0:T(8,128)S(1)} fusion(bf16[8,256,8,128]{1,3,2,0:T(8,128)(2,1)} %bitcast.12, f32[8,8,8,256]{3,2,1,0:T(8,128)S(1)} %get-tuple-element.8, f32[8,8,8]{2,1,0:T(8,128)S(1)} %broadcast_maximum_fusion, pred[8,256]{1,0:T(8,128)(4,1)S(1)} %iota_compare_fusion.5), kind=kOutput, calls=%fused_computation.16 | convolution fusion | flops 33947648 | bytes 4984832 | tf_op jit(solution)/shard_map/rgjp,rpgd->rgjd/dot_general | solution.py:355
  33.0 0.2 copy.37
  33.2 0.3 convert_reduce_fusion
  33.4 0.1 copy.35
  33.5 0.2 copy.36
  33.7 0.2 copy.34
  33.9 0.0 copy-done
  33.9 0.0 copy-done.5
  33.9 0.2 select_reduce_fusion.1
  34.1 0.1 fusion.refs_0_
  34.2 0.1 fusion.2.refs_4_
  34.3 19.3 %all-gather.2.cloned.1.call-done.refs_2_ = bf16[128,8192]{1,0:T(8,128)(2,1)} async-done(((bf16[8,8192]{1,0:T(8,128)(2,1)}), bf16[128,8192]{1,0:T(8,128)(2,1)}) %all-gather.2.cloned.1.call-update) | async-done | bytes 2097168 | tf_op jit(solution)/shard_map/all_gather | solution.py:362
  53.7 0.0 copy-done.1
  53.7 0.0 copy-start.2
  53.7 1.6 %copy-done.2 = bf16[128,8192]{1,0:T(8,128)(2,1)S(1)} copy-done((bf16[128,8192]{1,0:T(8,128)(2,1)S(1)}, bf16[128,8192]{1,0:T(8,128)(2,1)}, u32[]{:S(2)}) %copy-start.2) | copy-done | bytes 2097176
  55.2 58.9 %shard_map.73 = bf16[8,8192]{1,0:T(8,128)(2,1)S(1)} custom-call(f32[16,8,640]{2,1,0:T(8,128)S(1)} %fusion.refs_0_, bf16[512,8192]{1,0:T(8,128)(2,1)} %refs_1_.1, bf16[128,8192]{1,0:T(8,128)(2,1)S(1)} %copy-done.2, bf16[512,2048]{1,0:T(8,128)(2,1)S(1)} %copy-done.1, f32[512,128]{1,0:T(8,128)S(1)} %fusion.2.refs_4_), custom_call_target="tpu_custom_call" | custom-call | tf_op jit(solution)/shard_map/pallas_call | solution.py:307
  114.1 0.7 copy.47
  (3 shorter events, 0.0 us)
Async XLA Ops:
  6.5 27.3 %copy-start = (s32[8192,1]{0,1:T(1,128)S(1)}, s32[8192,1]{0,1:T(1,128)}, u32[]{:S(2)}) copy-start(s32[8192,1]{0,1:T(1,128)} %param.11) | copy-start | bytes 98308
  6.5 47.1 %all-gather.2.cloned.1.call-start = ((), (), s32[]{:S(2)}) async-start(), calls=%async_computation | async-start | bytes 2228224 | tf_op jit(solution)/shard_map/all_gather | solution.py:362
  19.7 6.6 %copy-start.4 = (s32[8]{0:T(128)S(1)}, s32[8]{0:T(128)}, u32[]{:S(2)}) copy-start(s32[8]{0:T(128)} %param.9) | copy-start | bytes 100
  19.7 6.6 %copy-start.3 = (bf16[8,8192]{1,0:T(8,128)(2,1)S(1)}, bf16[8,8192]{1,0:T(8,128)(2,1)}, u32[]{:S(2)}) copy-start(bf16[8,8192]{1,0:T(8,128)(2,1)} %param.7) | copy-start | bytes 393220
  29.3 4.6 %copy-start.5 = (s32[128]{0:T(128)S(1)}, s32[128]{0:T(128)}, u32[]{:S(2)}) copy-start(s32[128]{0:T(128)} %param.12) | copy-start | bytes 1540
  29.3 24.4 %copy-start.1 = (bf16[512,2048]{1,0:T(8,128)(2,1)S(1)}, bf16[512,2048]{1,0:T(8,128)(2,1)}, u32[]{:S(2)}) copy-start(bf16[512,2048]{1,0:T(8,128)(2,1)} %refs_3_.1) | copy-start | bytes 6291460
  53.7 1.6 %copy-start.2 = (bf16[128,8192]{1,0:T(8,128)(2,1)S(1)}, bf16[128,8192]{1,0:T(8,128)(2,1)}, u32[]{:S(2)}) copy-start(bf16[128,8192]{1,0:T(8,128)(2,1)} %all-gather.2.cloned.1.call-done.refs_2_) | copy-start | bytes 6291460
Sparse Core Ops, SparseCore 0:
  9.5 44.0 all-gather.1

commit v4 on v3

--- a/solution.py
+++ b/solution.py
@@ -56,8 +56,14 @@
     def _(g):
         keys = image_ref[:, pl.ds(pl.multiple_of(g * HD, HD), HD)]
         vals = image_ref[:, pl.ds(pl.multiple_of((KVH + g) * HD, HD), HD)].T
+        pairs = []
+        for j in range(per_group // 2):
+            cols = pl.ds(pl.multiple_of((g * (per_group // 2) + j) * HD, HD), HD)
+            both = query_ref[:, :, cols].astype(jnp.float32)
+            rows = both.shape[1] // 2
+            pairs.append([both[:, h * rows:(h + 1) * rows].reshape(n * rows, HD).astype(jnp.bfloat16) for h in (0, 1)])
         for j in range(per_group):
-            q = query_ref[:, pl.ds(pl.multiple_of((g * per_group + j) * HD, HD), HD)]
+            q = pairs[j % (per_group // 2)][j // (per_group // 2)]
             s = lax.dot_general(keys, q, (((1,), (1,)), ((), ())), preferred_element_type=jnp.float32)
             s = s * (1.0 / math.sqrt(HD)) + bias_ref[...]
             top = jnp.maximum(jnp.max(s, axis=0, keepdims=True), 0.1 * low_fill)
@@ -135,11 +141,57 @@
     return [copy for k in range(steps) for c in range(2) for copy in copies(c, k)]
 
 
+def cache_slot(n, r, heads_ref, cache, live_ref, att):
+    per_dev = QH // n
+    per_group = QH // KVH
+    lane = lax.broadcasted_iota(jnp.int32, (per_group, HD), 1)
+    head = lax.broadcasted_iota(jnp.int32, (per_group, HD), 0) % per_dev
+    for g in range(KVH):
+        q = heads_ref[r, pl.ds(g * per_group, per_group), :].astype(jnp.bfloat16)
+        s = lax.dot_general(q, cache[r, :, pl.ds(g * HD, HD)], (((1,), (1,)), ((), ())),
+                            preferred_element_type=jnp.float32)
+        s = s * (1.0 / math.sqrt(HD)) + live_ref[pl.ds(r, 1), :]
+        top = jnp.max(s, axis=1, keepdims=True)
+        w = jnp.exp(s - top).astype(jnp.bfloat16)
+        total = jnp.sum(w.astype(jnp.float32), axis=1, keepdims=True)
+        part = jnp.dot(w, cache[r, :, pl.ds((KVH + g) * HD, HD)], preferred_element_type=jnp.float32)
+        stats = jnp.where(lane == head, top, 0.0) + jnp.where(lane == head + 64, total, 0.0)
+        for d in range(per_group // per_dev):
+            dst = g * (per_group // per_dev) + d
+            for i in range(per_dev):
+                at = d * per_dev + i
+                att[dst, i, pl.ds(r, 1), :] = part[at:at + 1]
+            att[dst, per_dev, pl.ds(r, 1), :] = jnp.sum(
+                stats[d * per_dev:(d + 1) * per_dev], axis=0, keepdims=True)
+
+
+def gather_copies(n, c, k, query_ref, every, send_sem, recv_sem):
+    me = lax.axis_index("tp")
+    bits = list(range(n.bit_length() - 1))
+    order = bits[:0:-1] + bits[:1] if c == 0 else bits[1:2] + bits[:1:-1] + bits[:1]
+    base = me
+    for b in order[:k]:
+        base = base - bit_of(me, b) * (1 << b)
+    peer = me + (1 - 2 * bit_of(me, order[k])) * (1 << order[k])
+    wide = every.shape[2] // 2
+    cols = pl.ds(c * wide, wide)
+    copies = []
+    for j in range(1 << k):
+        at = base + sum([((j >> i) & 1) * (1 << b) for i, b in enumerate(order[:k])])
+        slot = (1 << k) - 1 + j
+        copies.append(pltpu.make_async_remote_copy(
+            src_ref=query_ref.at[:, cols] if k == 0 else every.at[at, :, cols], dst_ref=every.at[at, :, cols],
+            send_sem=send_sem.at[c, slot], recv_sem=recv_sem.at[c, slot],
+            device_id={"tp": peer}, device_id_type=pl.DeviceIdType.MESH))
+    return copies
+
+
 def project_kernel(n, fused, *refs):
     if fused:
-        (att_ref, weight_ref, query_ref, image_ref, bias_ref, out_ref, weight, got, acc, sent, landed,
+        (query_ref, weight_ref, heads_ref, cache_ref, live_ref, image_ref, bias_ref, out_ref, weight, got, acc, sent, landed,
          weight_sem, att_send, att_recv, send_sem, recv_sem,
-         num, stat, num_sent, num_got, stat_sent, stat_got, head_send, head_recv) = refs
+         num, stat, num_sent, num_got, stat_sent, stat_got, head_send, head_recv,
+         att_ref, every, cache, cache_sem, query_send, query_recv) = refs
     else:
         (att_ref, weight_ref, out_ref, weight, got, acc, sent, landed,
          weight_sem, att_send, att_recv, send_sem, recv_sem) = refs
@@ -147,6 +199,14 @@
     width = out_ref.shape[1] // CHUNKS
     steps = n.bit_length() - 1
     orders = chunk_orders(n)
+    rows = out_ref.shape[0]
+    if fused:
+        def cache_load(r):
+            return pltpu.make_async_copy(cache_ref.at[r], cache.at[r], cache_sem.at[r])
+
+        @pl.loop(0, rows)
+        def _(r):
+            cache_load(r).start()
     loads = []
     for c in range(CHUNKS):
         cols = pl.ds(c * width, width)
@@ -167,15 +227,34 @@
             src_ref=att_ref.at[dst], dst_ref=got.at[me], send_sem=att_send.at[o], recv_sem=att_recv.at[o],
             device_id={"tp": dst}, device_id_type=pl.DeviceIdType.MESH)
 
+    started = []
+    if fused:
+        every[me] = query_ref[...]
+        per_step = -(-rows // steps)
+        for k in range(steps):
+            for c in range(2):
+                copies = gather_copies(n, c, k, query_ref, every, query_send, query_recv)
+                for copy in copies:
+                    copy.start()
+                started = started + copies
+
+            @pl.loop(min(rows, k * per_step), min(rows, (k + 1) * per_step))
+            def _(r):
+                cache_load(r).wait()
+                cache_slot(n, r, heads_ref, cache, live_ref, att_ref)
+
+            for c in range(2):
+                for copy in gather_copies(n, c, k, query_ref, every, query_send, query_recv):
+                    copy.wait_recv()
+
     @pl.loop(1, n)
     def _(o):
         att_copy(o).start()
 
     got[me] = att_ref[me]
-    started = []
     if fused:
-        image_heads(n, query_ref, image_ref, bias_ref, num, stat)
-        started = sum_heads(n, num, stat, num_sent, num_got, stat_sent, stat_got, head_send, head_recv)
+        image_heads(n, every, image_ref, bias_ref, num, stat)
+        started = started + sum_heads(n, num, stat, num_sent, num_got, stat_sent, stat_got, head_send, head_recv)
 
     @pl.loop(1, n)
     def _(o):
@@ -184,19 +263,18 @@
             src_ref=att_ref.at[src], dst_ref=got.at[src], send_sem=att_send.at[o], recv_sem=att_recv.at[o],
             device_id={"tp": src}, device_id_type=pl.DeviceIdType.MESH).wait_recv()
 
-    rows = got.shape[1]
     if fused:
         per_dev = QH // n
-        cached = got[...].reshape(n * rows, got.shape[2]).T
-        depth = per_dev * HD
+        stats = got[:, per_dev].reshape(n * rows, HD).T
         pieces = []
         for h in range(per_dev):
             c, i = h // (per_dev // 2), h % (per_dev // 2)
-            ct, cs = cached[depth + h:depth + h + 1], cached[depth + 64 + h:depth + 65 + h]
+            cached = got[:, h].reshape(n * rows, HD).T
+            ct, cs = stats[h:h + 1], stats[64 + h:65 + h]
             it, isum = stat[c, me, pl.ds(i, 1), :], stat[c, me, pl.ds(4 + i, 1), :]
             top = jnp.maximum(ct, it)
             ce, ie = jnp.exp(ct - top), jnp.exp(it - top)
-            total = cached[h * HD:(h + 1) * HD] * ce + num[c, me, pl.ds(i * HD, HD), :] * ie
+            total = cached * ce + num[c, me, pl.ds(i * HD, HD), :] * ie
             pieces.append((total / (cs * ce + isum * ie)).T)
         att = jnp.concatenate(pieces, axis=1).astype(jnp.bfloat16)
     else:
@@ -286,11 +364,12 @@
 
 
 def project(by_owner, out_weight, n, image=()):
-    rows = by_owner.shape[1]
+    rows = by_owner.shape[0] // 2 if image else by_owner.shape[1]
     model = out_weight.shape[1]
     depth = out_weight.shape[0]
     steps = n.bit_length() - 1
     extra = []
+    got = (n, QH // n + 1, rows, HD) if image else by_owner.shape
     if image:
         half = depth // 2
         every = n * rows
@@ -303,16 +382,22 @@
             pltpu.VMEM((2, n - 1, 8, every), jnp.float32),
             pltpu.SemaphoreType.DMA((2, steps, 2)),
             pltpu.SemaphoreType.DMA((2, steps, 2)),
+            pltpu.VMEM(got, jnp.float32),
+            pltpu.VMEM((n,) + by_owner.shape, jnp.bfloat16),
+            pltpu.VMEM(image[1].shape, jnp.bfloat16),
+            pltpu.SemaphoreType.DMA((rows,)),
+            pltpu.SemaphoreType.DMA((2, n - 1)),
+            pltpu.SemaphoreType.DMA((2, n - 1)),
         ]
     return pl.pallas_call(
         functools.partial(project_kernel, n, bool(image)),
         out_shape=jax.ShapeDtypeStruct((rows, model), jnp.bfloat16),
         in_specs=[pl.BlockSpec(memory_space=pltpu.VMEM), pl.BlockSpec(memory_space=pl.ANY)]
-        + [pl.BlockSpec(memory_space=pltpu.VMEM)] * len(image),
+        + [pl.BlockSpec(memory_space=pl.ANY if i == 1 else pltpu.VMEM) for i in range(len(image))],
         out_specs=pl.BlockSpec(memory_space=pltpu.VMEM),
         scratch_shapes=[
             pltpu.VMEM((depth, model), jnp.bfloat16),
-            pltpu.VMEM(by_owner.shape, jnp.float32),
+            pltpu.VMEM(got, jnp.float32),
             pltpu.VMEM((n, rows, model), jnp.float32),
             pltpu.VMEM((n // 2, 2 * rows, model), jnp.bfloat16),
             pltpu.VMEM((n // 2, 2 * rows, model), jnp.bfloat16),
@@ -341,6 +426,17 @@
     row_slot = jnp.sum(
         jnp.where(my_rows[:, None] == req_iota[None, :], slot_of_request[None, :], 0), axis=1
     )
+    per_dev = QH // tp_size
+    if per_dev % 2 == 0 and per_dev <= QH // KVH:
+        live = row_slot[:, None] == req_iota[None, :]
+        bias = jnp.where(live, 0.0, low_fill).astype(jnp.float32)
+        per_group = QH // KVH
+        split = queries.reshape(local_req, KVH, 2, per_group // 2 * HD)
+        stacked = jnp.transpose(split, (2, 0, 1, 3)).reshape(2 * local_req, QH * HD // 2)
+        heads = queries.reshape(local_req, QH, HD).astype(jnp.float32)
+        cache_bias = jnp.where(
+            jnp.arange(CACHE, dtype=jnp.int32)[None, :] < cache_len[:, None], 0.0, low_fill).astype(jnp.float32)
+        return project(stacked, out_weight, tp_size, (heads, cache_kv, cache_bias, image_kv, bias))
     grouped = queries.reshape(local_req, KVH, QH // KVH, HD)
     cache_keys = cache_kv[:, :, :kv_width].reshape(local_req, CACHE, KVH, HD)
     cache_vals = cache_kv[:, :, kv_width:].reshape(local_req, CACHE, KVH, HD)
@@ -355,19 +451,6 @@
     cache_num = jnp.einsum(
         "rgjp,rpgd->rgjd", cache_weights, cache_vals, preferred_element_type=jnp.float32
     )
-    per_dev = QH // tp_size
-    if per_dev % 2 == 0 and per_dev <= QH // KVH:
-        live = row_slot[:, None] == req_iota[None, :]
-        bias = jnp.where(live, 0.0, low_fill).astype(jnp.float32)
-        every = lax.all_gather(queries, "tp", axis=0, tiled=True)
-
-        def spare(x):
-            x = x.reshape(local_req, tp_size, per_dev)
-            return jnp.pad(x, ((0, 0), (0, 0), (0, 64 - per_dev)))
-
-        packed = jnp.concatenate(
-            [cache_num.reshape(local_req, tp_size, per_dev * HD), spare(cache_top), spare(cache_sum)], axis=2)
-        return project(jnp.transpose(packed, (1, 0, 2)), out_weight, tp_size, (every, image_kv, bias))
     row_iota = jnp.arange(img_local, dtype=jnp.int32)
     earlier = (my_rows[:, None] == my_rows[None, :]) & (row_iota[None, :] < row_iota[:, None])
     row_rank = jnp.sum(earlier.astype(jnp.int32), axis=1)

time: 122 us -> 90.2 us (0.74)
  Pallas kernels: 58.9 us -> 83.2 us
  waiting for transfers between devices: 20 us -> 0 us
  local copies, waits for them, and re-layouts: 22 us -> 3.98 us
  between operations: 13.4 us -> 0.03 us
  matrix products: 6.48 us -> 0 us
  other arithmetic: 0.8 us -> 2.68 us
    pallas_call x1, Pallas kernels: 58.9 us -> 83.2 us  [project(): pl.pallas_call(functools.partial(project_kernel, n, bool(image)), out_sha...]
    all_gather x1 -> x0, waiting for transfers between devices: 19.3 us -> none  [per_device(): every = lax.all_gather(queries, 'tp', axis=0, tiled=True)]
    unnamed x15 -> x6, local copies, waits for them, and re-layouts: 15.3 us -> 3.06 us
    dot_general x2 -> x0, matrix products: 6.48 us -> none  [the longest x1 3.56 us: per_device(): jnp.einsum('rgjp,rpgd->rgjd', cache_weights, cache_vals, preferred_elemen...]
    slice x1 -> x0, local copies, waits for them, and re-layouts: 5.97 us -> none  [per_device(): cache_vals = cache_kv[:, :, kv_width:].reshape(local_req, CACHE, KVH, HD)]
  transfers between devices with their start and end apart: 1 -> 0, of which waited for: 1 -> 0; matrix products, arithmetic and copies ran while one was open for 22% -> 0% of each run, Pallas kernels for 0% -> 0%
where the time goes in v4:
time: 90.2 us; the launch traced here: 89.9 us
  Pallas kernels  83.2 us (92%)
  local copies, waits for them, and re-layouts  3.98 us (4%)
  other arithmetic  2.68 us (3%)
    pallas_call x1, Pallas kernels, project(): pl.pallas_call(functools.partial(project_kernel, n, bool(image)), out_sha...  83.2 us
    unnamed x6, local copies, waits for them, and re-layouts  3.06 us

profile of v4, /device:TPU:0, one launch (start us, length us, event | category | flops | bytes accessed | tf_op | source)
XLA Modules:
  0.0 89.9 jit_solution(16522074273226402311)
XLA Ops:
  0.0 0.0 copy-start
  0.0 0.8 copy-done
  0.8 0.9 select_reduce_fusion
  1.6 0.1 fusion.refs_6_
  1.8 0.9 %convert_bitcast_fusion = f32[1,8,64,128]{3,1,2,0:T(8,128)S(1)} fusion(bf16[8,8192]{1,0:T(8,128)(2,1)} %param.7), kind=kLoop, calls=%fused_computation.1 | loop fusion | flops 65536 | bytes 393216
  2.7 0.1 copy.12
  2.8 0.9 %copy.9 = bf16[8,8,2,512]{3,0,1,2:T(8,128)(2,1)S(1)} copy(bf16[8,8,2,512]{3,0,2,1:T(8,128)(2,1)} %bitcast.12) | data formatting | bytes 262144 | tf_op jit(solution)/shard_map/reshape | solution.py:434
  3.7 0.7 fusion.1.refs_4_
  4.4 0.0 copy-start.1
  4.4 1.6 %copy-done.1 = bf16[512,2048]{1,0:T(8,128)(2,1)S(1)} copy-done((bf16[512,2048]{1,0:T(8,128)(2,1)S(1)}, bf16[512,2048]{1,0:T(8,128)(2,1)}, u32[]{:S(2)}) %copy-start.1) | copy-done | bytes 2097176
  6.0 83.2 %shard_map.73 = bf16[8,8192]{1,0:T(8,128)(2,1)S(1)} custom-call(bf16[16,4096]{1,0:T(8,128)(2,1)S(1)} %bitcast.11, bf16[512,8192]{1,0:T(8,128)(2,1)} %refs_1_.1, f32[8,64,128]{2,1,0:T(8,128)S(1)} %bitcast.10, bf16[8,256,2048]{2,1,0:T(8,128)(2,1)} %refs_3_.1, f32[8,256]{1,0:T(8,128)S(1)} %fusion.1.refs_4_, bf16[512,2048]{1,0:T(8,128)(2,1)S(1)} %copy-done.1, ...), custom_call_target="tpu_custom_call" | custom-call | tf_op jit(solution)/shard_map/pallas_call | solution.py:392
  89.2 0.7 copy.14
  (1 shorter events, 0.0 us)
Async XLA Ops:
  0.0 0.8 copy-start
  4.4 1.6 %copy-start.1 = (bf16[512,2048]{1,0:T(8,128)(2,1)S(1)}, bf16[512,2048]{1,0:T(8,128)(2,1)}, u32[]{:S(2)}) copy-start(bf16[512,2048]{1,0:T(8,128)(2,1)} %refs_5_.1) | copy-start | bytes 6291460
